TPU v7x, 128 devices: a whole 4x4x4 slice. The times are simulated.
128 devices in a mesh: ctx: 32 (over z, y, core), fsdp: 4 (over x).
Axes of the slice: x: 4, y: 4, z: 4, core: 2. Of those that a mesh axis runs over, the one named last changes fastest.
Arguments:
- tokens: bfloat16 [4, 4096, 576], P('fsdp', 'ctx'), may hold values from -6 to 6
- pairing: int32 [64], replicated, may hold values from 0 to 63, as said below
- cotangent: float32 [4, 4096, 576], P('fsdp', 'ctx'), may hold values from -6 to 6
- w_query: bfloat16 [2, 576, 576], P(None, 'fsdp'), may hold values from -0.25 to 0.25
- key_projection_weight: bfloat16 [2, 576, 192], P(None, 'fsdp'), may hold values from -0.25 to 0.25
- value_projection_weight: bfloat16 [2, 576, 192], P(None, 'fsdp'), may hold values from -0.25 to 0.25
- w_out: bfloat16 [2, 576, 576], P(None, 'fsdp'), may hold values from -6 to 6
- w_gate: bfloat16 [2, 576, 1536], P(None, None, 'fsdp'), may hold values from -0.25 to 0.25
- w_up: bfloat16 [2, 576, 1536], P(None, None, 'fsdp'), may hold values from -0.25 to 0.25
- w_down: bfloat16 [2, 1536, 576], P(None, 'fsdp'), may hold values from -0.15625 to 0.15625
- attn_gain: bfloat16 [2, 576], P(None, 'fsdp'), may hold values from 0.099609375 to 1.8984375
- ffn_gain: bfloat16 [2, 576], P(None, 'fsdp'), may hold values from 0.099609375 to 1.8984375
Outputs:
- out: float32 [4, 4096, 576], P('fsdp', 'ctx')
- d_tokens: float32 [4, 4096, 576], P('fsdp', 'ctx')
- d_w_query: float32 [2, 576, 576], P(None, 'fsdp')
- d_w_key: float32 [2, 576, 192], P(None, 'fsdp')
- d_w_value: float32 [2, 576, 192], P(None, 'fsdp')
- d_w_out: float32 [2, 576, 576], P(None, 'fsdp')
- d_w_gate: float32 [2, 576, 1536], P(None, None, 'fsdp')
- d_w_up: float32 [2, 576, 1536], P(None, None, 'fsdp')
- d_w_down: float32 [2, 1536, 576], P(None, 'fsdp')
- d_attn_gain: float32 [2, 576], P(None, 'fsdp')
- d_ffn_gain: float32 [2, 576], P(None, 'fsdp')
Inputs may be any that keep to these rules, and one draw needn't show every extreme that they name: `pairing`: every value appears once. Entries 2 c and 2 c + 1 are the position blocks of storage blocks 2 c and 2 c + 1; they add up to 63.
All inputs are finite; a program needn't handle non-finite values.
Results may differ from a plain program's by a relative error of at most 0.03.
Values may be sent and summed in bfloat16 or wider, within the bound.
No kernel may reach another device: no remote copies, remote signals or barrier semaphores. Data moves between devices by JAX's collectives and lax.ppermute only.
A program may use at most 128 MiB of HBM per device.

v0:
```python
import jax
import jax.numpy as jnp
from jax import lax
from jax.sharding import PartitionSpec as P

QUERY_HEADS = 9
KEY_VALUE_HEADS = 3
HEAD_SIZE = 64


epsilon = 1e-05
rope_base = 100000.0
negative = -1e30


def angles(positions):
    half_dim = HEAD_SIZE // 2
    frequency = rope_base ** (-(jnp.arange(half_dim, dtype=jnp.float32) * 2.0 / HEAD_SIZE))
    return positions.astype(jnp.float32)[:, None] * frequency[None, :]


def rotary_apply(values, angle_table):
    half_dim = values.shape[-1] // 2
    cos_part = jnp.cos(angle_table)[:, None, :]
    sin_part = jnp.sin(angle_table)[:, None, :]
    first_half = values[..., :half_dim]
    second_half = values[..., half_dim:]
    return jnp.concatenate(
        [
            first_half * cos_part - second_half * sin_part,
            second_half * cos_part + first_half * sin_part,
        ],
        axis=-1,
    )


def normalize(stream, gain):
    return stream * lax.rsqrt(jnp.mean(stream * stream, axis=-1, keepdims=True) + epsilon) * gain


def activate(gate_pre, up_pre):
    return gate_pre * jax.nn.sigmoid(gate_pre) * up_pre


def apply_projection(incoming_rows, weight_matrix):
    return jnp.einsum(
        "aqu,uo->aqo", incoming_rows, weight_matrix, preferred_element_type=jnp.float32
    )


def back_project(gradient_tree, weight_matrix):
    return jnp.einsum(
        "cza,ga->czg", gradient_tree, weight_matrix, preferred_element_type=jnp.float32
    )


def outer_sum(incoming_rows, gradient_tree):
    return jnp.einsum(
        "jpc,jpf->cf", incoming_rows, gradient_tree, preferred_element_type=jnp.float32
    )


def local(
    tokens,
    pairing,
    cotangent,
    w_query,
    key_projection_weight,
    value_projection_weight,
    w_out,
    w_gate,
    w_up,
    w_down,
    attn_gain,
    ffn_gain,
):
    sequence_count, count_of_rows, model_width = tokens.shape
    half_rows = count_of_rows // 2
    every_row_set = count_of_rows * lax.axis_size("ctx")
    repeat_heads = QUERY_HEADS // KEY_VALUE_HEADS
    score_scale = HEAD_SIZE ** (-0.5)
    key_block = min(512, every_row_set)
    key_steps = every_row_set // key_block
    layer_count = w_query.shape[0]
    ctx_index = lax.axis_index("ctx")
    own_blocks = lax.dynamic_slice_in_dim(pairing, 2 * ctx_index, 2)
    offsets = jnp.arange(half_rows, dtype=jnp.int32)
    query_pos = (own_blocks[:, None] * half_rows + offsets[None, :]).reshape(count_of_rows)
    key_pos = (pairing[:, None] * half_rows + offsets[None, :]).reshape(every_row_set)
    rotary_angles = angles(query_pos)
    inverse_angles = -rotary_angles
    head_layout = (sequence_count, KEY_VALUE_HEADS, repeat_heads, count_of_rows)

    def scores(query_fifth, every_key_row, key_step):
        key_row_set = lax.dynamic_slice_in_dim(every_key_row, key_step * key_block, key_block, 1)
        key_places = lax.dynamic_slice_in_dim(key_pos, key_step * key_block, key_block, 0)
        raw = (
            jnp.einsum(
                "sqgrd,skgd->sgrqk", query_fifth, key_row_set, preferred_element_type=jnp.float32
            )
            * score_scale
        )
        return jnp.where(key_places[None, :] <= query_pos[:, None], raw, negative)

    stream = tokens.astype(jnp.float32)
    saved = []
    for layer_index in range(layer_count):
        query_weight, key_matrix, value_matrix, out_weight, gain_one, gain_two = (
            lax.all_gather(w_query[layer_index], "fsdp", axis=0, tiled=True),
            lax.all_gather(key_projection_weight[layer_index], "fsdp", axis=0, tiled=True),
            lax.all_gather(value_projection_weight[layer_index], "fsdp", axis=0, tiled=True),
            lax.all_gather(w_out[layer_index], "fsdp", axis=0, tiled=True),
            lax.all_gather(attn_gain[layer_index], "fsdp", axis=0, tiled=True),
            lax.all_gather(ffn_gain[layer_index], "fsdp", axis=0, tiled=True),
        )
        normalized_rows = normalize(stream, gain_one.astype(jnp.float32)).astype(jnp.bfloat16)
        query_row_set = rotary_apply(
            apply_projection(normalized_rows, query_weight).reshape(
                sequence_count, count_of_rows, QUERY_HEADS, HEAD_SIZE
            ),
            rotary_angles,
        ).astype(jnp.bfloat16)
        fresh_keys = rotary_apply(
            apply_projection(normalized_rows, key_matrix).reshape(
                sequence_count, count_of_rows, KEY_VALUE_HEADS, HEAD_SIZE
            ),
            rotary_angles,
        ).astype(jnp.bfloat16)
        value_new = apply_projection(normalized_rows, value_matrix).astype(jnp.bfloat16)
        flattened_keys, flattened_values = (
            lax.all_gather(
                fresh_keys.reshape(sequence_count, count_of_rows, KEY_VALUE_HEADS * HEAD_SIZE),
                "ctx",
                axis=1,
                tiled=True,
            ),
            lax.all_gather(value_new, "ctx", axis=1, tiled=True),
        )
        every_key_row = flattened_keys.reshape(
            sequence_count, every_row_set, KEY_VALUE_HEADS, HEAD_SIZE
        )
        every_value_row = flattened_values.reshape(
            sequence_count, every_row_set, KEY_VALUE_HEADS, HEAD_SIZE
        )
        query_fifth = query_row_set.reshape(
            sequence_count, count_of_rows, KEY_VALUE_HEADS, repeat_heads, HEAD_SIZE
        )

        def softmax_stats(carry, key_step):
            running_max, running_sum = carry
            score_block = scores(query_fifth, every_key_row, key_step)
            new_max = jnp.maximum(running_max, jnp.max(score_block, axis=-1))
            running_sum = running_sum * jnp.exp(running_max - new_max) + jnp.sum(
                jnp.exp(score_block - new_max[..., None]), axis=-1
            )
            return ((new_max, running_sum), None)

        initial = (
            jnp.full(head_layout, negative, jnp.float32),
            jnp.zeros(head_layout, jnp.float32),
        )
        (running_max, running_sum), unused = lax.scan(softmax_stats, initial, jnp.arange(key_steps))
        log_total = running_max + jnp.log(running_sum)

        def mix_values(accum, key_step):
            score_block = scores(query_fifth, every_key_row, key_step)
            probs_b = jnp.exp(score_block - log_total[..., None]).astype(jnp.bfloat16)
            value_row_set = lax.dynamic_slice_in_dim(
                every_value_row, key_step * key_block, key_block, 1
            )
            return (
                accum
                + jnp.einsum(
                    "sgrqk,skgd->sqgrd", probs_b, value_row_set, preferred_element_type=jnp.float32
                ),
                None,
            )

        attention_output, unused = lax.scan(
            mix_values,
            jnp.zeros(
                (sequence_count, count_of_rows, KEY_VALUE_HEADS, repeat_heads, HEAD_SIZE),
                jnp.float32,
            ),
            jnp.arange(key_steps),
        )
        attention_output = attention_output.reshape(
            sequence_count, count_of_rows, QUERY_HEADS * HEAD_SIZE
        )
        attended_b = attention_output.astype(jnp.bfloat16)
        middle = stream + apply_projection(attended_b, out_weight)
        normed_two = normalize(middle, gain_two.astype(jnp.float32)).astype(jnp.bfloat16)
        gate_weight, up_weight, down_weight = (
            lax.all_gather(w_gate[layer_index], "fsdp", axis=1, tiled=True),
            lax.all_gather(w_up[layer_index], "fsdp", axis=1, tiled=True),
            lax.all_gather(w_down[layer_index], "fsdp", axis=0, tiled=True),
        )
        ffn_rows = normed_two
        gate_pre = apply_projection(ffn_rows, gate_weight)
        up_pre = apply_projection(ffn_rows, up_weight)
        hidden = activate(gate_pre, up_pre).astype(jnp.bfloat16)
        branch = apply_projection(hidden, down_weight)
        saved.append(
            (
                stream,
                normalized_rows,
                query_fifth,
                every_key_row,
                every_value_row,
                log_total,
                attention_output,
                middle,
                ffn_rows,
                gate_pre,
                up_pre,
                hidden,
                query_weight,
                key_matrix,
                value_matrix,
                out_weight,
                gain_one,
                gain_two,
                gate_weight,
                up_weight,
                down_weight,
            )
        )
        stream = middle + branch
    stream_grad = cotangent
    layer_grads = [None] * layer_count
    for layer_index in reversed(range(layer_count)):
        (
            stream_in,
            normalized_rows,
            query_fifth,
            every_key_row,
            every_value_row,
            log_total,
            attention_output,
            middle,
            ffn_rows,
            gate_pre,
            up_pre,
            hidden,
            query_weight,
            key_matrix,
            value_matrix,
            out_weight,
            gain_one,
            gain_two,
            gate_weight,
            up_weight,
            down_weight,
        ) = saved[layer_index]
        query_weight, key_matrix, value_matrix, out_weight, gain_one, gain_two = (
            lax.all_gather(w_query[layer_index], "fsdp", axis=0, tiled=True),
            lax.all_gather(key_projection_weight[layer_index], "fsdp", axis=0, tiled=True),
            lax.all_gather(value_projection_weight[layer_index], "fsdp", axis=0, tiled=True),
            lax.all_gather(w_out[layer_index], "fsdp", axis=0, tiled=True),
            lax.all_gather(attn_gain[layer_index], "fsdp", axis=0, tiled=True),
            lax.all_gather(ffn_gain[layer_index], "fsdp", axis=0, tiled=True),
        )
        branch_grad = stream_grad.astype(jnp.bfloat16)
        hidden_grad = back_project(branch_grad, down_weight)
        grad_down = outer_sum(hidden, branch_grad)
        unused, activate_back = jax.vjp(activate, gate_pre, up_pre)
        gate_grad, up_grad = activate_back(hidden_grad)
        gate_grad = gate_grad.astype(jnp.bfloat16)
        up_grad = up_grad.astype(jnp.bfloat16)
        grad_gate = outer_sum(ffn_rows, gate_grad)
        grad_up = outer_sum(ffn_rows, up_grad)
        normed_two_grad = back_project(gate_grad, gate_weight) + back_project(up_grad, up_weight)
        grad_gate, grad_up, grad_down = (
            lax.psum_scatter(
                grad_gate.astype(jnp.bfloat16), "fsdp", scatter_dimension=1, tiled=True
            ).astype(jnp.float32),
            lax.psum_scatter(
                grad_up.astype(jnp.bfloat16), "fsdp", scatter_dimension=1, tiled=True
            ).astype(jnp.float32),
            lax.psum_scatter(
                grad_down.astype(jnp.bfloat16), "fsdp", scatter_dimension=0, tiled=True
            ).astype(jnp.float32),
        )
        unused, norm_back = jax.vjp(normalize, middle, gain_two.astype(jnp.float32))
        middle_part, grad_gain_two = norm_back(normed_two_grad)
        middle_grad = stream_grad + middle_part
        attn_branch_grad = middle_grad.astype(jnp.bfloat16)
        attended_b = attention_output.astype(jnp.bfloat16)
        grad_out = outer_sum(attended_b, attn_branch_grad)
        attended_grad = (
            back_project(attn_branch_grad, out_weight)
            .astype(jnp.bfloat16)
            .reshape(sequence_count, count_of_rows, KEY_VALUE_HEADS, repeat_heads, HEAD_SIZE)
        )
        row_delta = jnp.sum(
            attended_grad.astype(jnp.float32)
            * attention_output.reshape(
                sequence_count, count_of_rows, KEY_VALUE_HEADS, repeat_heads, HEAD_SIZE
            ),
            axis=-1,
        )
        row_delta = jnp.transpose(row_delta, (0, 2, 3, 1))

        def backward_sweep(query_accum, key_step):
            score_block = scores(query_fifth, every_key_row, key_step)
            softmax_p = jnp.exp(score_block - log_total[..., None])
            key_row_set = lax.dynamic_slice_in_dim(
                every_key_row, key_step * key_block, key_block, 1
            )
            value_row_set = lax.dynamic_slice_in_dim(
                every_value_row, key_step * key_block, key_block, 1
            )
            value_part = jnp.einsum(
                "sgrqk,sqgrd->skgd",
                softmax_p.astype(jnp.bfloat16),
                attended_grad,
                preferred_element_type=jnp.float32,
            )
            prob_grad = jnp.einsum(
                "sqgrd,skgd->sgrqk",
                attended_grad,
                value_row_set,
                preferred_element_type=jnp.float32,
            )
            score_grad = (softmax_p * (prob_grad - row_delta[..., None])).astype(
                jnp.bfloat16
            ) * score_scale
            query_accum = query_accum + jnp.einsum(
                "sgrqk,skgd->sqgrd", score_grad, key_row_set, preferred_element_type=jnp.float32
            )
            key_part = jnp.einsum(
                "sgrqk,sqgrd->skgd", score_grad, query_fifth, preferred_element_type=jnp.float32
            )
            return (query_accum, (key_part, value_part))

        query_grad, (key_pieces, value_pieces) = lax.scan(
            backward_sweep,
            jnp.zeros(
                (sequence_count, count_of_rows, KEY_VALUE_HEADS, repeat_heads, HEAD_SIZE),
                jnp.float32,
            ),
            jnp.arange(key_steps),
        )
        gathered_keys = jnp.moveaxis(key_pieces, 0, 1).reshape(
            sequence_count, every_row_set, KEY_VALUE_HEADS * HEAD_SIZE
        )
        gathered_values = jnp.moveaxis(value_pieces, 0, 1).reshape(
            sequence_count, every_row_set, KEY_VALUE_HEADS * HEAD_SIZE
        )
        key_gradient, value_grad = (
            lax.psum_scatter(
                gathered_keys.astype(jnp.bfloat16), "ctx", scatter_dimension=1, tiled=True
            ).astype(jnp.float32),
            lax.psum_scatter(
                gathered_values.astype(jnp.bfloat16), "ctx", scatter_dimension=1, tiled=True
            ).astype(jnp.float32),
        )
        query_pre = (
            rotary_apply(
                query_grad.reshape(sequence_count, count_of_rows, QUERY_HEADS, HEAD_SIZE),
                inverse_angles,
            )
            .astype(jnp.bfloat16)
            .reshape(sequence_count, count_of_rows, QUERY_HEADS * HEAD_SIZE)
        )
        key_pre = (
            rotary_apply(
                key_gradient.reshape(sequence_count, count_of_rows, KEY_VALUE_HEADS, HEAD_SIZE),
                inverse_angles,
            )
            .astype(jnp.bfloat16)
            .reshape(sequence_count, count_of_rows, KEY_VALUE_HEADS * HEAD_SIZE)
        )
        value_pre = value_grad.astype(jnp.bfloat16)
        grad_query = outer_sum(normalized_rows, query_pre)
        grad_key = outer_sum(normalized_rows, key_pre)
        grad_value = outer_sum(normalized_rows, value_pre)
        normed_grad = (
            back_project(query_pre, query_weight)
            + back_project(key_pre, key_matrix)
            + back_project(value_pre, value_matrix)
        )
        unused, norm_back = jax.vjp(normalize, stream_in, gain_one.astype(jnp.float32))
        stream_part, grad_gain_one = norm_back(normed_grad)
        stream_grad = middle_grad + stream_part
        shares = (
            lax.psum_scatter(
                grad_query.astype(jnp.bfloat16), "fsdp", scatter_dimension=0, tiled=True
            ).astype(jnp.float32),
            lax.psum_scatter(
                grad_key.astype(jnp.bfloat16), "fsdp", scatter_dimension=0, tiled=True
            ).astype(jnp.float32),
            lax.psum_scatter(
                grad_value.astype(jnp.bfloat16), "fsdp", scatter_dimension=0, tiled=True
            ).astype(jnp.float32),
            lax.psum_scatter(
                grad_out.astype(jnp.bfloat16), "fsdp", scatter_dimension=0, tiled=True
            ).astype(jnp.float32),
            lax.psum_scatter(
                grad_gain_one.astype(jnp.bfloat16), "fsdp", scatter_dimension=0, tiled=True
            ).astype(jnp.float32),
            lax.psum_scatter(
                grad_gain_two.astype(jnp.bfloat16), "fsdp", scatter_dimension=0, tiled=True
            ).astype(jnp.float32),
        )
        layer_grads[layer_index] = shares + (grad_gate, grad_up, grad_down)
    stacked = [
        jnp.stack([layer_grads[index_layer][member] for index_layer in range(layer_count)])
        for member in range(9)
    ]
    (
        sum_query,
        sum_key,
        sum_value,
        sum_out,
        sum_gain_one,
        sum_gain_two,
        sum_gate,
        sum_up,
        sum_down,
    ) = (
        lax.psum(stacked[0].astype(jnp.bfloat16), "ctx").astype(jnp.float32),
        lax.psum(stacked[1].astype(jnp.bfloat16), "ctx").astype(jnp.float32),
        lax.psum(stacked[2].astype(jnp.bfloat16), "ctx").astype(jnp.float32),
        lax.psum(stacked[3].astype(jnp.bfloat16), "ctx").astype(jnp.float32),
        lax.psum(stacked[4].astype(jnp.bfloat16), "ctx").astype(jnp.float32),
        lax.psum(stacked[5].astype(jnp.bfloat16), "ctx").astype(jnp.float32),
        lax.psum(stacked[6].astype(jnp.bfloat16), "ctx").astype(jnp.float32),
        lax.psum(stacked[7].astype(jnp.bfloat16), "ctx").astype(jnp.float32),
        lax.psum(stacked[8].astype(jnp.bfloat16), "ctx").astype(jnp.float32),
    )
    return (
        stream,
        stream_grad,
        sum_query,
        sum_key,
        sum_value,
        sum_out,
        sum_gate,
        sum_up,
        sum_down,
        sum_gain_one,
        sum_gain_two,
    )


def solution(mesh):
    return jax.shard_map(
        local,
        mesh=mesh,
        in_specs=(
            P("fsdp", "ctx", None),
            P(),
            P("fsdp", "ctx", None),
            P(None, "fsdp", None),
            P(None, "fsdp", None),
            P(None, "fsdp", None),
            P(None, "fsdp", None),
            P(None, None, "fsdp"),
            P(None, None, "fsdp"),
            P(None, "fsdp", None),
            P(None, "fsdp"),
            P(None, "fsdp"),
        ),
        out_specs=(
            P("fsdp", "ctx", None),
            P("fsdp", "ctx", None),
            P(None, "fsdp", None),
            P(None, "fsdp", None),
            P(None, "fsdp", None),
            P(None, "fsdp", None),
            P(None, None, "fsdp"),
            P(None, None, "fsdp"),
            P(None, "fsdp", None),
            P(None, "fsdp"),
            P(None, "fsdp"),
        ),
        check_vma=False,
    )
```

profile of v0, /device:TPU:1, one launch (start us, length us, event | category | flops | bytes accessed | tf_op | source)
XLA Modules:
  0.0 1494.0 jit_solution(1672170889360383700)
XLA Ops:
  88.5 39.3 %while.78 = (s32[]{:T(128)}, f32[1,3,3,128]{3,2,1,0:T(4,128)S(1)}, f32[1,3,3,128]{3,2,1,0:T(4,128)S(1)}, s32[8]{0:T(128)S(1)}, s32[4096]{0:T(1024)}, /*index=5*/...) while((s32[]{:T(128)}, f32[1,3,3,128]{3,2,1,0:T(4,128)S(1)}, ...), condition=%wide.region_4.5_spmd.clone, body=%wide.region_1.4_spmd.clone.sunk | while | flops 79697672 | bytes 5327570 | solution.py:162
  133.8 45.0 %while.79 = (s32[]{:T(128)}, f32[1,128,3,3,64]{1,4,3,2,0:T(8,128)}, s32[8]{0:T(128)S(1)}, bf16[1,4096,3,64]{1,3,2,0:T(8,128)(2,1)}, s32[4096]{0:T(1024)}, /*inde...) while((s32[]{:T(128)}, f32[1,128,3,3,64]{1,4,3,2,0:T(8,128)}, ...), condition=%wide.region_6.7_spmd.clone, body=%wide.region_5.6_spmd.clone.sunk | while | flops 153567360 | bytes 1276116 | solution.py:179
  196.2 26.7 %all-gather.41.cloned.1.call-done = bf16[1,1536,576]{1,2,0:T(8,128)(2,1)} async-done(((bf16[1,384,576]{1,2,0:T(8,128)(2,1)}), bf16[1,1536,576]{1,2,0:T(8,128)(2,1)}) %all-gather.41.cloned.1.call-update) | async-done | bytes 1769488 | tf_op jit(solution)/shard_map/all_gather | solution.py:196
  270.0 35.7 %all-gather.33.cloned.1.call-done = bf16[1,4096,192]{1,2,0:T(8,128)(2,1)} async-done(((bf16[1,128,192]{1,2,0:T(8,128)(2,1)}), bf16[1,4096,192]{1,2,0:T(8,128)(2,1)}) %all-gather.33.cloned.1.call-update) | async-done | bytes 1572880 | tf_op jit(solution)/shard_map/all_gather | solution.py:131
  305.7 39.3 %while.80 = (s32[]{:T(128)}, f32[1,3,3,128]{3,2,1,0:T(4,128)S(1)}, f32[1,3,3,128]{3,2,1,0:T(4,128)S(1)}, s32[8]{0:T(128)S(1)}, s32[4096]{0:T(1024)}, /*index=5*/...) while((s32[]{:T(128)}, f32[1,3,3,128]{3,2,1,0:T(4,128)S(1)}, ...), condition=%wide.region_12.13_spmd.clone, body=%wide.region_9.12_spmd.clone.sunk | while | flops 79697672 | bytes 5327570 | solution.py:162
  351.8 38.7 %while.81 = (s32[]{:T(128)}, f32[1,128,3,3,64]{1,4,3,2,0:T(8,128)S(1)}, s32[8]{0:T(128)S(1)}, bf16[1,4096,3,64]{1,3,2,0:T(8,128)(2,1)}, s32[4096]{0:T(1024)}, /*...) while((s32[]{:T(128)}, ...), condition=%wide.region_14.15_spmd.clone, body=%wide.region_13.14_spmd.clone.sunk | while | flops 153567360 | bytes 1276116 | solution.py:179
  420.5 104.1 %while.82 = (s32[]{:T(128)}, f32[1,128,3,3,64]{1,4,3,2,0:T(8,128)}, bf16[8,1,512,3,64]{2,4,3,1,0:T(8,128)(2,1)}, bf16[8,1,512,3,64]{2,4,3,1,0:T(8,128)(2,1)}, s3...) while((s32[]{:T(128)}, f32[1,128,3,3,64]{1,4,3,2,0:T(8,128)}, ...), condition=%wide.region_19.20_spmd.clone, body=%wide.region_18.19_spmd.clone.sunk | while | flops 384188544 | bytes 16354137 | solution.py:336
  557.7 59.8 %reduce-scatter.55.cloned.1.call-done = bf16[128,192]{1,0:T(8,128)(2,1)} async-done(((bf16[4096,192]{1,0:T(8,128)(2,1)}), bf16[128,192]{1,0:T(8,128)(2,1)}) %reduce-scatter.55.cloned.1.call-update) | async-done | bytes 49168
  618.6 80.5 %reduce-scatter.57.cloned.1.call-done = bf16[128,192]{1,0:T(8,128)(2,1)} async-done(((bf16[4096,192]{1,0:T(8,128)(2,1)}), bf16[128,192]{1,0:T(8,128)(2,1)}) %reduce-scatter.57.cloned.1.call-update) | async-done | bytes 49168
  710.1 95.8 %while.83 = (s32[]{:T(128)}, f32[1,128,3,3,64]{1,4,3,2,0:T(8,128)}, bf16[8,1,512,3,64]{2,4,3,1,0:T(8,128)(2,1)}, bf16[8,1,512,3,64]{2,4,3,1,0:T(8,128)(2,1)}, s3...) while((s32[]{:T(128)}, f32[1,128,3,3,64]{1,4,3,2,0:T(8,128)}, ...), condition=%wide.region_26.27_spmd.clone, body=%wide.region_25.26_spmd.clone.sunk | while | flops 384188544 | bytes 15154445 | solution.py:336
  856.3 43.5 %reduce-scatter.59.cloned.1.call-done = bf16[128,192]{1,0:T(8,128)(2,1)} async-done(((bf16[4096,192]{1,0:T(8,128)(2,1)}), bf16[128,192]{1,0:T(8,128)(2,1)}) %reduce-scatter.59.cloned.1.call-update) | async-done | bytes 49168
  903.0 78.4 %reduce-scatter.61.cloned.1.call-done = bf16[128,192]{1,0:T(8,128)(2,1)} async-done(((bf16[4096,192]{1,0:T(8,128)(2,1)}), bf16[128,192]{1,0:T(8,128)(2,1)}) %reduce-scatter.61.cloned.1.call-update) | async-done | bytes 49168
  1014.4 29.4 %reduce-scatter.69.cloned.1.call-done = bf16[384,576]{1,0:T(8,128)(2,1)} async-done(((bf16[1536,576]{1,0:T(8,128)(2,1)}), bf16[384,576]{1,0:T(8,128)(2,1)}) %reduce-scatter.69.cloned.1.call-update) | async-done | bytes 442384
  1045.1 29.4 %reduce-scatter.73.cloned.1.call-done = bf16[384,576]{1,0:T(8,128)(2,1)} async-done(((bf16[1536,576]{1,0:T(8,128)(2,1)}), bf16[384,576]{1,0:T(8,128)(2,1)}) %reduce-scatter.73.cloned.1.call-update) | async-done | bytes 442384
  1098.2 25.0 %reduce-scatter.39.cloned.1.call-done = bf16[144,576]{1,0:T(8,128)(2,1)} async-done(((bf16[576,576]{1,0:T(8,128)(2,1)}), bf16[144,576]{1,0:T(8,128)(2,1)}) %reduce-scatter.39.cloned.1.call-update) | async-done | bytes 165904 | tf_op jit(solution)/shard_map/reduce_scatter | solution.py:387
  1125.0 23.0 %reduce-scatter.53.cloned.1.call-done = bf16[144,576]{1,0:T(8,128)(2,1)} async-done(((bf16[576,576]{1,0:T(8,128)(2,1)}), bf16[144,576]{1,0:T(8,128)(2,1)}) %reduce-scatter.53.cloned.1.call-update) | async-done | bytes 165904 | tf_op jit(solution)/shard_map/reduce_scatter | solution.py:396
  1148.0 25.0 %reduce-scatter.51.cloned.1.call-done = bf16[144,576]{1,0:T(8,128)(2,1)} async-done(((bf16[576,576]{1,0:T(8,128)(2,1)}), bf16[144,576]{1,0:T(8,128)(2,1)}) %reduce-scatter.51.cloned.1.call-update) | async-done | bytes 165904 | tf_op jit(solution)/shard_map/reduce_scatter | solution.py:396
  1195.2 23.4 %reduce-scatter.43.cloned.1.call-done = bf16[144,192]{1,0:T(8,128)(2,1)} async-done(((bf16[576,192]{1,0:T(8,128)(2,1)}), bf16[144,192]{1,0:T(8,128)(2,1)}) %reduce-scatter.43.cloned.1.call-update) | async-done | bytes 55312 | tf_op jit(solution)/shard_map/reduce_scatter | solution.py:390
  1241.9 22.8 %reduce-scatter.47.cloned.1.call-done = bf16[144,192]{1,0:T(8,128)(2,1)} async-done(((bf16[576,192]{1,0:T(8,128)(2,1)}), bf16[144,192]{1,0:T(8,128)(2,1)}) %reduce-scatter.47.cloned.1.call-update) | async-done | bytes 55312 | tf_op jit(solution)/shard_map/reduce_scatter | solution.py:393
  1266.3 31.3 %reduce-scatter.63.cloned.1.call-done = bf16[384,576]{1,0:T(8,128)(2,1)} async-done(((bf16[1536,576]{1,0:T(8,128)(2,1)}), bf16[384,576]{1,0:T(8,128)(2,1)}) %reduce-scatter.63.cloned.1.call-update) | async-done | bytes 442384
  1298.9 29.4 %reduce-scatter.67.cloned.1.call-done = bf16[384,576]{1,0:T(8,128)(2,1)} async-done(((bf16[1536,576]{1,0:T(8,128)(2,1)}), bf16[384,576]{1,0:T(8,128)(2,1)}) %reduce-scatter.67.cloned.1.call-update) | async-done | bytes 442384
  1329.5 29.5 %reduce-scatter.71.cloned.1.call-done = bf16[384,576]{1,0:T(8,128)(2,1)} async-done(((bf16[1536,576]{1,0:T(8,128)(2,1)}), bf16[384,576]{1,0:T(8,128)(2,1)}) %reduce-scatter.71.cloned.1.call-update) | async-done | bytes 442384
  1374.7 65.1 %all-reduce.8 = (bf16[2,144]{1,0:T(2,128)(2,1)S(1)}, bf16[2,144]{1,0:T(2,128)(2,1)S(1)}) all-reduce(bf16[2,144]{1,0:T(2,128)(2,1)S(1)} %get-tuple-element.765, bf16[2,144]{1,0:T(2,128)(2,1)S(1)} %get-tuple-element.766), channel_id=1, replica_groups=mesh['ctx'=32,'fsdp'=4] {'ctx'}, use_global_device_ids=true, to_apply=%region_55.56 | all-reduce | flops 576 | bytes 2304 | tf_op jit(solution)/shard_map/psum | solution.py:426
  1441.8 34.8 %all-reduce.14.cloned.1.call-done = (bf16[2,144,576]{2,1,0:T(8,128)(2,1)}, bf16[2,144,192]{2,1,0:T(8,128)(2,1)}, bf16[2,144,192]{2,1,0:T(8,128)(2,1)}, bf16[2,14...) async-done(((bf16[2,144,576]{2,1,0:T(8,128)(2,1)}, bf16[2,144,192]{2,1,0:T(8,128)(2,1)}, ...) | async-done | bytes 3538960 | tf_op jit(solution)/shard_map/psum | solution.py:422
  (1258 shorter events, 748.4 us)
Async XLA Ops:
  51.4 171.5 %all-gather.41.cloned.1.call-start = ((), (), s32[]{:S(2)}) async-start(), calls=%async_computation.31 | async-start | bytes 2211840 | tf_op jit(solution)/shard_map/all_gather | solution.py:196
  52.7 214.0 %all-gather.49.cloned.1.call-start = ((), (), s32[]{:S(2)}) async-start(), calls=%async_computation.35 | async-start | bytes 2211840 | tf_op jit(solution)/shard_map/all_gather | solution.py:196
  53.3 252.4 %all-gather.33.cloned.1.call-start = ((), (), s32[]{:S(2)}) async-start(), calls=%async_computation.19 | async-start | bytes 1622016 | tf_op jit(solution)/shard_map/all_gather | solution.py:131
  237.0 154.3 %all-gather.47.cloned.1.call-start = ((), (), s32[]{:S(2)}) async-start(), calls=%async_computation.34 | async-start | bytes 2211840 | tf_op jit(solution)/shard_map/all_gather | solution.py:195
  237.7 173.0 %all-gather.45.cloned.1.call-start = ((), (), s32[]{:S(2)}) async-start(), calls=%async_computation.33 | async-start | bytes 2211840 | tf_op jit(solution)/shard_map/all_gather | solution.py:194
  238.3 379.2 %reduce-scatter.55.cloned.1.call-start = ((), (), s32[]{:S(2)}) async-start(), calls=%async_computation.36 | async-start | bytes 2162688
  540.1 159.1 %reduce-scatter.57.cloned.1.call-start = ((), (), s32[]{:S(2)}) async-start(), calls=%async_computation.37 | async-start | bytes 2162688
  555.6 344.2 %reduce-scatter.59.cloned.1.call-start = ((), (), s32[]{:S(2)}) async-start(), calls=%async_computation.38 | async-start | bytes 2162688
  821.4 160.0 %reduce-scatter.61.cloned.1.call-start = ((), (), s32[]{:S(2)}) async-start(), calls=%async_computation.39 | async-start | bytes 2162688
  837.0 176.2 %reduce-scatter.65.cloned.1.call-start = ((), (), s32[]{:S(2)}) async-start(), calls=%async_computation.41 | async-start | bytes 2457600
  841.0 202.8 %reduce-scatter.69.cloned.1.call-start = ((), (), s32[]{:S(2)}) async-start(), calls=%async_computation.43 | async-start | bytes 2457600
  844.9 229.5 %reduce-scatter.73.cloned.1.call-start = ((), (), s32[]{:S(2)}) async-start(), calls=%async_computation.45 | async-start | bytes 2457600
  848.9 249.3 %reduce-scatter.41.cloned.1.call-start = ((), (), s32[]{:S(2)}) async-start(), calls=%async_computation.21 | async-start | bytes 921600 | tf_op jit(solution)/shard_map/reduce_scatter | solution.py:387
  851.1 272.1 %reduce-scatter.39.cloned.1.call-start = ((), (), s32[]{:S(2)}) async-start(), calls=%async_computation.20 | async-start | bytes 921600 | tf_op jit(solution)/shard_map/reduce_scatter | solution.py:387
  852.6 295.4 %reduce-scatter.53.cloned.1.call-start = ((), (), s32[]{:S(2)}) async-start(), calls=%async_computation.27 | async-start | bytes 921600 | tf_op jit(solution)/shard_map/reduce_scatter | solution.py:396
  853.9 319.1 %reduce-scatter.51.cloned.1.call-start = ((), (), s32[]{:S(2)}) async-start(), calls=%async_computation.26 | async-start | bytes 921600 | tf_op jit(solution)/shard_map/reduce_scatter | solution.py:396
  855.2 340.0 %reduce-scatter.45.cloned.1.call-start = ((), (), s32[]{:S(2)}) async-start(), calls=%async_computation.23 | async-start | bytes 368640 | tf_op jit(solution)/shard_map/reduce_scatter | solution.py:390
  856.3 362.4 %reduce-scatter.43.cloned.1.call-start = ((), (), s32[]{:S(2)}) async-start(), calls=%async_computation.22 | async-start | bytes 368640 | tf_op jit(solution)/shard_map/reduce_scatter | solution.py:390
  901.9 339.9 %reduce-scatter.49.cloned.1.call-start = ((), (), s32[]{:S(2)}) async-start(), calls=%async_computation.25 | async-start | bytes 368640 | tf_op jit(solution)/shard_map/reduce_scatter | solution.py:393
  903.0 361.7 %reduce-scatter.47.cloned.1.call-start = ((), (), s32[]{:S(2)}) async-start(), calls=%async_computation.24 | async-start | bytes 368640 | tf_op jit(solution)/shard_map/reduce_scatter | solution.py:393
  983.5 314.1 %reduce-scatter.63.cloned.1.call-start = ((), (), s32[]{:S(2)}) async-start(), calls=%async_computation.40 | async-start | bytes 2457600
  986.5 341.7 %reduce-scatter.67.cloned.1.call-start = ((), (), s32[]{:S(2)}) async-start(), calls=%async_computation.42 | async-start | bytes 2457600
  990.4 368.6 %reduce-scatter.71.cloned.1.call-start = ((), (), s32[]{:S(2)}) async-start(), calls=%async_computation.44 | async-start | bytes 2457600
  994.4 482.2 %all-reduce.14.cloned.1.call-start = ((), (), s32[]{:S(2)}) async-start(), calls=%async_computation.46 | async-start | bytes 7372800 | tf_op jit(solution)/shard_map/psum | solution.py:422
  (289 other events, 3818.9 us)
Sparse Core Ops, SparseCore 0:
  38.2 49.4 all-gather.30
  90.5 43.2 all-gather.34
  136.1 26.9 all-gather.36
  165.2 28.0 all-gather.38
  194.8 28.0 all-gather.40
  224.5 34.2 all-gather.48
  260.9 44.7 all-gather.32
  308.4 43.2 all-gather.42
  354.0 26.9 all-gather.46
  382.6 28.0 all-gather.44
  540.2 77.3 reduce-scatter.54
  620.9 78.1 reduce-scatter.56
  821.6 78.2 reduce-scatter.58
  903.2 78.1 reduce-scatter.60
  983.7 29.4 reduce-scatter.64
  1015.4 28.3 reduce-scatter.68
  1046.1 28.3 reduce-scatter.72
  1101.1 21.9 reduce-scatter.38
  1126.0 21.9 reduce-scatter.52
  1151.0 21.9 reduce-scatter.50
  1267.0 30.6 reduce-scatter.62
  1299.9 28.3 reduce-scatter.66
  1330.7 28.3 reduce-scatter.70
  1364.6 111.9 all-reduce.13
  (5 shorter events, 101.0 us)
where the time goes:
time: 1510 us; the launch traced here: 1490 us
  waiting for transfers between devices  753 us (50%)
  matrix products  257 us (17%)
  local copies, waits for them, and re-layouts  187 us (12%)
  blocking collectives  169 us (11%)
  other arithmetic  74.7 us (5%)
  loops' own time  35.2 us (2%)
  between operations  17.6 us (1%)
    unnamed x39, waiting for transfers between devices  432 us
    unnamed x273, local copies, waits for them, and re-layouts  93.1 us
    psum x1, blocking collectives, local(): lax.psum(stacked[4].astype(jnp.bfloat16), 'ctx').astype(jnp.float32)  65.1 us
    reduce_scatter x2, waiting for transfers between devices, local(): lax.psum_scatter(grad_out.astype(jnp.bfloat16), 'fsdp', scatter_dimension...  48 us
    reduce_scatter x2, waiting for transfers between devices, local(): lax.psum_scatter(grad_query.astype(jnp.bfloat16), 'fsdp', scatter_dimensi...  47.5 us
    dot_general x32, matrix products, scores(): jnp.einsum('sqgrd,skgd->sgrqk', query_fifth, key_row_set, preferred_eleme...  46.8 us
    reduce_scatter x2, waiting for transfers between devices, local(): lax.psum_scatter(grad_value.astype(jnp.bfloat16), 'fsdp', scatter_dimensi...  44.4 us
    reduce_scatter x2, waiting for transfers between devices, local(): lax.psum_scatter(grad_key.astype(jnp.bfloat16), 'fsdp', scatter_dimension...  43.8 us
  transfers between devices with their start and end apart: 29, of which 25 were waited for; matrix products, arithmetic and copies ran while one was open for 16% of the time, Pallas kernels for 0%

commit v1 on v0

v1 whole, which is shorter than its diff:
```python
import functools

import jax
import jax.numpy as jnp
from jax import lax
from jax.experimental import pallas as pl
from jax.experimental.pallas import tpu as pltpu
from jax.sharding import PartitionSpec as P

D = 576
HQ = 9
HK = 3
HD = 64
FF = 1536
BLK = 64
ROWS = 128
SEQ = 4096
KW = 192
CH = 256
EPS = 1e-05
BASE = 100000.0
NEG = -1e30
F32 = jnp.float32
BF = jnp.bfloat16
AXES = ("ctx", "fsdp")
OFFS = (0, -1, 1, 2)


def nn(a, b):
    return lax.dot_general(a, b, (((1,), (0,)), ((), ())), preferred_element_type=F32)


def nt(a, b):
    return lax.dot_general(a, b, (((1,), (1,)), ((), ())), preferred_element_type=F32)


def tn(a, b):
    return lax.dot_general(a, b, (((0,), (0,)), ((), ())), preferred_element_type=F32)


def pairs(move):
    found = []
    for z in range(4):
        for y in range(4):
            for c in range(2):
                for x in range(4):
                    a, b, e, f = move(z, y, c, x)
                    found.append(
                        (
                            ((z * 4 + y) * 2 + c) * 4 + x,
                            (((a % 4) * 4 + b % 4) * 2 + e) * 4 + f % 4,
                        )
                    )
    return found


def send(value, move):
    return lax.ppermute(value, AXES, pairs(move))


def plane(stage, k):
    def move(z, y, c, x):
        if (c + stage) % 2 == 0:
            return z, y + k, c, x
        return z + k, y, c, x

    return move


def along_x(k):
    return lambda z, y, c, x: (z, y, c, x + k)


def other_core(z, y, c, x):
    return z, y, 1 - c, x


def gather_stage(value, shift):
    return [value, send(value, shift(1)), send(value, shift(-1)), send(value, shift(2))]


def scatter_stage(parts, shift):
    return [
        parts[0],
        send(parts[1], shift(-1)),
        send(parts[2], shift(1)),
        send(parts[3], shift(2)),
    ]


def total(parts):
    return sum(p.astype(F32) for p in parts)


def gather_plane(value):
    first = jnp.concatenate(gather_stage(value, lambda k: plane(0, k)), 0)
    own = jnp.concatenate(gather_stage(first, lambda k: plane(1, k)), 0)
    return own, send(own, other_core)


def scatter_plane(own, other):
    both = total([own, send(other, other_core)]).astype(BF)
    parts = both.reshape((4, 512) + own.shape[1:])
    one = total(scatter_stage([parts[j] for j in range(4)], lambda k: plane(1, k))).astype(BF)
    one = one.reshape((4, 128) + own.shape[1:])
    return scatter_stage([one[j] for j in range(4)], lambda k: plane(0, k))


def reduce_all(own, other):
    half = total([own, send(other, other_core)]).astype(BF)
    part = total(scatter_stage([half[j] for j in range(4)], along_x)).astype(BF)
    part = total(gather_stage(part, lambda k: plane(0, k))).astype(BF)
    part = total(gather_stage(part, lambda k: plane(1, k))).astype(BF)
    return part, send(part, other_core)


def call(body, outs, args, smem=0, scratch=(), us=5.0, name=None):
    specs = [pl.BlockSpec(memory_space=pltpu.SMEM)] * smem
    specs += [pl.BlockSpec(memory_space=pltpu.VMEM)] * (len(args) - smem)
    return pl.pallas_call(
        body,
        out_shape=[jax.ShapeDtypeStruct(s, d) for s, d in outs],
        in_specs=specs,
        out_specs=[pl.BlockSpec(memory_space=pltpu.VMEM)] * len(outs),
        scratch_shapes=list(scratch),
        compiler_params=pltpu.CompilerParams(vmem_limit_bytes=58 * 1024 * 1024),
        cost_estimate=pl.CostEstimate(
            flops=int(us * 1.1e9), bytes_accessed=1000000, transcendentals=0
        ),
        name=name,
    )(*args)


def spin(v, cos, sin, back=False):
    lane = lax.broadcasted_iota(jnp.int32, (v.shape[0], 128), 1)
    low = (lane % 64) < 32
    pieces = []
    for j in range(v.shape[1] // 128):
        part = v[:, 128 * j : 128 * j + 128]
        swapped = jnp.where(low, pltpu.roll(part, 96, 1), pltpu.roll(part, 32, 1))
        if back:
            pieces.append(part * cos - swapped * sin)
        else:
            pieces.append(part * cos + swapped * sin)
    return jnp.concatenate(pieces, 1)


def rms(x):
    return lax.rsqrt(jnp.mean(x * x, axis=-1, keepdims=True) + EPS)


def norm_back(x, gain, grad):
    r = rms(x)
    inner = jnp.mean(grad * gain * x, axis=-1, keepdims=True)
    d_x = r * gain * grad - x * (r * r * r * inner)
    d_gain = jnp.sum(grad * x * r, axis=0, keepdims=True)
    return d_x, d_gain


def project(normed, weight, cos, sin, q_ref, kv_ref):
    mixed = nn(normed, weight)
    turned = spin(mixed[:, :768], cos, sin)
    q_ref[...] = (turned[:, :D].astype(BF).astype(F32) * (HD**-0.5)).astype(BF)
    kv_ref[:, :KW] = turned[:, D:768].astype(BF)
    kv_ref[:, KW:] = mixed[:, 768:960].astype(BF)


def first_kernel(x_ref, tok, p0, p1, p2, p3, cos, sin, normed, q, kv, w, gains, tmp):
    for j, piece in enumerate((p0, p1, p2, p3)):
        owner = lax.rem(x_ref[0] + (OFFS[j] + 4), 4)
        tmp[pl.ds(pl.multiple_of(owner * 144, 16), 144), :] = piece[...]
    w[...] = tmp[:, :960]
    g = tmp[:, 896:1024].astype(F32).T
    gains[...] = g[64:72, :]
    x = tok[...].astype(F32)
    n = (x * rms(x) * g[64:65, :]).astype(BF)
    normed[...] = n
    project(n, w[...], cos[...], sin[...], q, kv)


def spread(src, dst, block):
    dst[...] = jnp.zeros(dst.shape, BF)
    for h in range(HQ):
        g = h // 3
        dst[HD * h : HD * h + HD, HD * g : HD * g + HD] = src[
            BLK * block : BLK * block + BLK, HD * h : HD * h + HD
        ]


def allowed(chunk, position):
    key = lax.broadcasted_iota(jnp.int32, (CH, D), 0) + chunk * CH
    query = (lax.broadcasted_iota(jnp.int32, (CH, D), 1) % BLK) + position * BLK
    return key <= query


def attend_kernel(tab, own_pos, q, kvo, kvt, kp, vp, ot, lse, att, qbd, acc, stat):
    def place(s, carry):
        for base, ref in ((0, kvo), (32, kvt)):
            at = pl.ds(pl.multiple_of(tab[base + s] * BLK, BLK), BLK)
            rows = ref[pl.ds(pl.multiple_of(s * BLK, BLK), BLK), :]
            kp[at, :] = rows[:, :KW]
            vp[at, :] = rows[:, KW:]
        return carry

    lax.fori_loop(0, 32, place, 0)
    for block in range(2):
        position = own_pos[block]
        spread(q, qbd, block)
        stat[0:1, :] = jnp.full((1, D), NEG, F32)
        stat[1:2, :] = jnp.zeros((1, D), F32)
        acc[...] = jnp.zeros((KW, D), F32)

        def step(i, masked):
            at = pl.ds(pl.multiple_of(i * CH, CH), CH)
            s = nt(kp[at, :], qbd[...])
            if masked:
                s = jnp.where(allowed(i, position), s, NEG)
            old = stat[0:1, :]
            new = jnp.maximum(old, jnp.max(s, axis=0, keepdims=True))
            p = jnp.exp(s - new)
            fade = jnp.exp(old - new)
            stat[0:1, :] = new
            stat[1:2, :] = stat[1:2, :] * fade + jnp.sum(p, axis=0, keepdims=True)
            acc[...] = acc[...] * fade + tn(vp[at, :], p.astype(BF))

        def loop(i, carry):
            step(i, False)
            return carry

        last = position // 4
        lax.fori_loop(0, last, loop, 0)
        step(last, True)
        result = acc[...] / stat[1:2, :]
        ot[block] = result
        lse[block] = jnp.broadcast_to(stat[0:1, :] + jnp.log(stat[1:2, :]), (8, D))
        turned = result.T
        for h in range(HQ):
            g = h // 3
            att[BLK * block : BLK * block + BLK, HD * h : HD * h + HD] = turned[
                HD * h : HD * h + HD, HD * g : HD * g + HD
            ].astype(BF)


def ffn_forward(n2, pieces):
    out = None
    for p in pieces:
        gate = nt(n2, p[0:KW, :])
        up = nt(n2, p[KW : 2 * KW, :])
        hidden = (gate * jax.nn.sigmoid(gate) * up).astype(BF)
        term = nn(hidden, p[2 * KW : 3 * KW, :])
        out = term if out is None else out + term
    return out


def middle_kernel(stream, att, wo, gains, gain_row, w0, w1, w2, w3, v0, v1, v2, v3, *rest):
    if len(rest) > 3:
        wqkv, cos, sin, middle_ref, n2_ref, out, normed, q, kv = rest
    else:
        middle_ref, n2_ref, out = rest
    middle = stream[...].astype(F32) + nn(att[...], wo[...])
    middle_ref[...] = middle
    n2 = (middle * rms(middle) * gains[gain_row + 1 : gain_row + 2, :]).astype(BF)
    n2_ref[...] = n2
    result = middle + ffn_forward(n2, (w0, w1, w2, w3, v0, v1, v2, v3))
    out[...] = result
    if len(rest) > 3:
        n = (result * rms(result) * gains[gain_row + 2 : gain_row + 3, :]).astype(BF)
        normed[...] = n
        project(n, wqkv[...], cos[...], sin[...], q, kv)


def ffn_back_kernel(
    gain_row, grad, middle, n2_ref, att, wo, gains, w0, w1, w2, w3, v0, v1, v2, v3,
    g_own, g_oth, mid_grad, d_out, d_wo, d_gain,
):
    g = grad[...]
    branch = g.astype(BF)
    n2 = n2_ref[...]
    n2_grad = None
    for j, p in enumerate((w0, w1, w2, w3, v0, v1, v2, v3)):
        dst = g_own if j < 4 else g_oth
        k = j % 4
        gate = nt(n2, p[0:KW, :])
        up = nt(n2, p[KW : 2 * KW, :])
        s = jax.nn.sigmoid(gate)
        hidden = (gate * s * up).astype(BF)
        hidden_grad = nt(branch, p[2 * KW : 3 * KW, :])
        gate_grad = (hidden_grad * up * s * (1.0 + gate * (1.0 - s))).astype(BF)
        up_grad = (hidden_grad * gate * s).astype(BF)
        dst[k, 0:KW, :] = tn(gate_grad, n2).astype(BF)
        dst[k, KW : 2 * KW, :] = tn(up_grad, n2).astype(BF)
        dst[k, 2 * KW : 3 * KW, :] = tn(hidden, branch).astype(BF)
        term = nn(gate_grad, p[0:KW, :]) + nn(up_grad, p[KW : 2 * KW, :])
        n2_grad = term if n2_grad is None else n2_grad + term
    part, gain_grad = norm_back(middle[...], gains[gain_row + 1 : gain_row + 2, :], n2_grad)
    m_grad = g + part
    mid_grad[...] = m_grad
    d_gain[...] = jnp.broadcast_to(gain_grad, (8, D))
    ab = m_grad.astype(BF)
    d_wo[...] = tn(att[...], ab).astype(BF)
    d_out[...] = nt(ab, wo[...]).astype(BF)


def attend_back_kernel(
    tab, own_pos, q, d_out, kp, vp, ot, lse, cos, sin, dkv_own, dkv_oth, dq_pre,
    qbd, dbd, dk, dv, dqt, flat,
):
    dk[...] = jnp.zeros(dk.shape, F32)
    dv[...] = jnp.zeros(dv.shape, F32)
    flat[:, D:] = jnp.zeros((ROWS, 64), F32)
    for block in range(2):
        position = own_pos[block]
        spread(q, qbd, block)
        spread(d_out, dbd, block)
        delta = jnp.sum(ot[block] * dbd[...].astype(F32).T, axis=0, keepdims=True)
        log_total = lse[block][0:1, :]
        dqt[...] = jnp.zeros((KW, D), F32)

        def step(i, masked):
            at = pl.ds(pl.multiple_of(i * CH, CH), CH)
            p = jnp.exp(nt(kp[at, :], qbd[...]) - log_total)
            if masked:
                p = jnp.where(allowed(i, position), p, 0.0)
            p_grad = nt(vp[at, :], dbd[...])
            s_grad = (p * (p_grad - delta)).astype(BF)
            dv[at, :] += nn(p.astype(BF), dbd[...])
            dk[at, :] += nn(s_grad, qbd[...])
            dqt[...] += tn(kp[at, :], s_grad)

        def loop(i, carry):
            step(i, False)
            return carry

        last = position // 4
        lax.fori_loop(0, last, loop, 0)
        step(last, True)
        turned = (dqt[...] * (HD**-0.5)).T
        for h in range(HQ):
            g = h // 3
            flat[BLK * block : BLK * block + BLK, HD * h : HD * h + HD] = turned[
                HD * h : HD * h + HD, HD * g : HD * g + HD
            ]
    dq_pre[...] = spin(flat[...], cos[...], sin[...], True)[:, :D].astype(BF)

    def place(s, carry):
        for base, ref in ((0, dkv_own), (32, dkv_oth)):
            at = pl.ds(pl.multiple_of(tab[base + s] * BLK, BLK), BLK)
            to = pl.ds(pl.multiple_of(s * BLK, BLK), BLK)
            ref[to, :] = jnp.concatenate([dk[at, :].astype(BF), dv[at, :].astype(BF)], 1)
        return carry

    lax.fori_loop(0, 32, place, 0)


def project_back_kernel(
    gain_row, place_ref, t0, t1, t2, t3, dq_pre, normed, stream, gains, wqkv, mid_grad,
    d_wo, d_gain_two, cos, sin, grad, g_own, g_oth, kbuf, full,
):
    x, c = place_ref[0], place_ref[1]
    dkv = t0[...].astype(F32) + t1[...].astype(F32) + t2[...].astype(F32) + t3[...].astype(F32)
    kbuf[:, :KW] = dkv[:, :KW]
    kbuf[:, KW:] = jnp.zeros((ROWS, 64), F32)
    dk_pre = spin(kbuf[...], cos[...], sin[...], True)[:, :KW].astype(BF)
    dqk = jnp.concatenate([dq_pre[...], dk_pre], 1)
    dv_pre = dkv[:, KW:].astype(BF)
    n = normed[...]
    full[0, :D, :] = tn(n, dqk).astype(BF)
    full[1, :D, :] = jnp.concatenate([tn(n, dv_pre).astype(BF), d_wo[...]], 1)
    n_grad = nt(jnp.concatenate([dqk, dv_pre], 1), wqkv[...])
    part, gain_grad = norm_back(stream[...].astype(F32), gains[gain_row : gain_row + 1, :], n_grad)
    grad[...] = mid_grad[...] + part
    full[0, D:, :] = jnp.zeros((16, 768), BF)
    full[1, D:, :] = jnp.zeros((16, 768), BF)
    full[0, D:, :D] = jnp.broadcast_to(gain_grad, (16, D)).astype(BF)
    full[1, D:, :D] = jnp.broadcast_to(d_gain_two[0:1, :], (16, D)).astype(BF)
    for j in range(4):
        owner = lax.rem(x + (OFFS[j] + 4), 4)
        at = pl.ds(pl.multiple_of(owner * 144, 16), 144)
        g_own[j, :144, :] = full[c, at, :]
        g_own[j, 144:, :] = full[c, D:, :]
        g_oth[j, :144, :] = full[1 - c, at, :]
        g_oth[j, 144:, :] = full[1 - c, D:, :]


def local(tokens, pairing, cotangent, w_query, w_key, w_value, w_out, w_gate, w_up, w_down, attn_gain, ffn_gain):
    ctx = lax.axis_index("ctx")
    x = lax.axis_index("fsdp")
    z, y, c = ctx // 8, (ctx // 2) % 4, ctx % 2

    gains_in = jnp.stack([attn_gain[0], ffn_gain[0], attn_gain[1], ffn_gain[1]], 1)
    bundle = jnp.concatenate(
        [w_query[0], w_key[0], w_value[0], gains_in, jnp.zeros((144, 60), BF)], 1
    )
    first_pieces = gather_stage(bundle, along_x)
    rest = jnp.concatenate([w_out[0], w_query[1], w_key[1], w_value[1], w_out[1]], 1)
    rest = lax.all_gather(rest, "fsdp", axis=0, tiled=True)
    wo = [rest[:, :D], rest[:, D + 960 :]]

    def halves(layer):
        parts = [
            lax.dynamic_slice_in_dim(m, KW * c, KW, 0)
            for m in (w_gate[layer].T, w_up[layer].T, w_down[layer])
        ]
        return jnp.concatenate(parts, 0)

    ffn = []
    for layer in range(2):
        own = gather_stage(halves(layer), along_x)
        ffn.append(own + [send(p, other_core) for p in own])

    spot = jnp.arange(16, dtype=jnp.int32)
    step = jnp.array(OFFS, jnp.int32)
    inner, outer = step[spot % 4], step[spot // 4]

    def owners(core):
        along_y = jnp.where(core == 0, inner, outer)
        along_z = jnp.where(core == 0, outer, inner)
        return ((z + along_z) % 4) * 8 + ((y + along_y) % 4) * 2 + core

    owner = jnp.concatenate([owners(c), owners(1 - c)])
    tab = pairing.reshape(32, 2)[owner].reshape(64)
    own_pos = lax.dynamic_slice_in_dim(pairing, 2 * ctx, 2)
    rows = (own_pos[:, None] * BLK + jnp.arange(BLK, dtype=jnp.int32)[None, :]).reshape(ROWS)
    frequency = BASE ** (-(jnp.arange(HD // 2, dtype=F32) * 2.0 / HD))
    angle = rows.astype(F32)[:, None] * frequency[None, :]
    cos1, sin1 = jnp.cos(angle), jnp.sin(angle)
    cos = jnp.concatenate([cos1] * 4, 1)
    sin = jnp.concatenate([-sin1, sin1] * 2, 1)
    place = jnp.stack([x, c]).astype(jnp.int32)

    act = (ROWS, D)
    stream0 = tokens[0]
    normed0, q0, kv0, wqkv0, gains = call(
        first_kernel,
        [(act, BF), (act, BF), ((ROWS, 384), BF), ((D, 960), BF), ((8, D), F32)],
        [place, stream0, *first_pieces, cos, sin],
        smem=1,
        scratch=[pltpu.VMEM((D, 1024), BF)],
        us=3.0,
        name="project_first",
    )

    def attend(q, kv):
        own, oth = gather_plane(kv)
        return call(
            attend_kernel,
            [
                ((SEQ, KW), BF),
                ((SEQ, KW), BF),
                ((2, KW, D), F32),
                ((2, 8, D), F32),
                (act, BF),
            ],
            [tab, own_pos, q, own, oth],
            smem=2,
            scratch=[pltpu.VMEM((D, KW), BF), pltpu.VMEM((KW, D), F32), pltpu.VMEM((8, D), F32)],
            us=12.0,
            name="attend",
        )

    kp0, vp0, ot0, lse0, att0 = attend(q0, kv0)
    wqkv1 = rest[:, D : D + 960]
    middle0, n20, stream1, normed1, q1, kv1 = call(
        lambda s, a, o, g, *r: middle_kernel(s, a, o, g, 0, *r),
        [(act, F32), (act, BF), (act, F32), (act, BF), (act, BF), ((ROWS, 384), BF)],
        [stream0, att0, wo[0], gains, *ffn[0], wqkv1, cos, sin],
        us=8.0,
        name="middle_first",
    )
    kp1, vp1, ot1, lse1, att1 = attend(q1, kv1)
    middle1, n21, out = call(
        lambda s, a, o, g, *r: middle_kernel(s, a, o, g, 2, *r),
        [(act, F32), (act, BF), (act, F32)],
        [stream1, att1, wo[1], gains, *ffn[1]],
        us=6.0,
        name="middle_last",
    )

    def back(layer, grad, middle, n2, att, q, kp, vp, ot, lse, normed, stream, wqkv):
        g_own, g_oth, mid_grad, d_out, d_wo, d_gain_two = call(
            functools.partial(ffn_back_kernel, 2 * layer),
            [
                ((4, D, D), BF),
                ((4, D, D), BF),
                (act, F32),
                (act, BF),
                ((D, D), BF),
                ((8, D), F32),
            ],
            [grad, middle, n2, att, wo[layer], gains, *ffn[layer]],
            us=10.0,
            name="ffn_back",
        )
        ffn_sums = reduce_all(g_own, g_oth)
        dkv_own, dkv_oth, dq_pre = call(
            attend_back_kernel,
            [((2048, 384), BF), ((2048, 384), BF), (act, BF)],
            [tab, own_pos, q, d_out, kp, vp, ot, lse, cos, sin],
            smem=2,
            scratch=[
                pltpu.VMEM((D, KW), BF),
                pltpu.VMEM((D, KW), BF),
                pltpu.VMEM((SEQ, KW), F32),
                pltpu.VMEM((SEQ, KW), F32),
                pltpu.VMEM((KW, D), F32),
                pltpu.VMEM((ROWS, 640), F32),
            ],
            us=20.0,
            name="attend_back",
        )
        terms = scatter_plane(dkv_own, dkv_oth)
        new_grad, a_own, a_oth = call(
            functools.partial(project_back_kernel, 2 * layer),
            [(act, F32), ((4, 160, 768), BF), ((4, 160, 768), BF)],
            [place, *terms, dq_pre, normed, stream, gains, wqkv, mid_grad, d_wo, d_gain_two, cos, sin],
            smem=1,
            scratch=[pltpu.VMEM((ROWS, 256), F32), pltpu.VMEM((2, D + 16, 768), BF)],
            us=5.0,
            name="project_back",
        )
        attn_sums = reduce_all(a_own, a_oth)
        return new_grad, ffn_sums, attn_sums

    grad1, ffn1, attn1 = back(
        1, cotangent[0], middle1, n21, att1, q1, kp1, vp1, ot1, lse1, normed1, stream1, wqkv1
    )
    grad0, ffn0, attn0 = back(
        0, grad1, middle0, n20, att0, q0, kp0, vp0, ot0, lse0, normed0, stream0, wqkv0
    )

    def ordered(sums):
        mine, theirs = (s.astype(F32) for s in sums)
        return jnp.where(c == 0, mine, theirs), jnp.where(c == 0, theirs, mine)

    results = []
    for ffn_sums, attn_sums in ((ffn0, attn0), (ffn1, attn1)):
        low, high = ordered(ffn_sums)
        both = jnp.concatenate([low.reshape(3, KW, D), high.reshape(3, KW, D)], 1)
        one, two = ordered(attn_sums)
        gain_at = lambda v: lax.dynamic_slice_in_dim(v[144, :D], 144 * x, 144, 0)
        results.append(
            (
                one[:144, :D],
                one[:144, D:],
                two[:144, :KW],
                two[:144, KW:],
                both[0].T,
                both[1].T,
                both[2],
                gain_at(one),
                gain_at(two),
            )
        )
    stacked = [jnp.stack([results[0][i], results[1][i]]) for i in range(9)]
    return (out[None], grad0[None], *stacked)


def solution(mesh):
    rows = P("fsdp", "ctx", None)
    wide = P(None, "fsdp", None)
    deep = P(None, None, "fsdp")
    flat = P(None, "fsdp")
    return jax.shard_map(
        local,
        mesh=mesh,
        in_specs=(rows, P(), rows, wide, wide, wide, wide, deep, deep, wide, flat, flat),
        out_specs=(rows, rows, wide, wide, wide, wide, deep, deep, wide, flat, flat),
        check_vma=False,
    )
```

time: 1510 us -> 591 us (0.39)
  waiting for transfers between devices: 753 us -> 241 us
  matrix products: 257 us -> 0 us
  blocking collectives: 169 us -> 0 us
  local copies, waits for them, and re-layouts: 187 us -> 54.4 us
  Pallas kernels: 0 us -> 129 us
  starting transfers between devices: 1.66 us -> 100 us
  loops' own time: 35.2 us -> 0 us
  other arithmetic: 74.7 us -> 42.6 us
    unnamed x39 -> x1, waiting for transfers between devices: 432 us -> 0.02 us
    dot_general x154 -> x0, matrix products: 257 us -> none  [the longest x32 46.8 us: scores(): jnp.einsum('sqgrd,skgd->sgrqk', query_fifth, key_row_set, preferred_eleme...]
    ppermute x0 -> x89, waiting for transfers between devices: none -> 241 us  [send(): return lax.ppermute(value, AXES, pairs(move))]
    reduce_scatter x8 -> x0, waiting for transfers between devices: 184 us -> none  [the longest x2 48 us: local(): lax.psum_scatter(grad_out.astype(jnp.bfloat16), 'fsdp', scatter_dimension...]
    pallas_call x0 -> x11, Pallas kernels: none -> 129 us  [call(): pl.pallas_call(body, out_shape=[jax.ShapeDtypeStruct(s, d) for s, d in ou...]
    all_gather x10 -> x1, waiting for transfers between devices: 102 us -> 0.01 us  [local(): rest = lax.all_gather(rest, 'fsdp', axis=0, tiled=True)]
    ppermute x0 -> x89, starting transfers between devices: none -> 100 us  [send(): return lax.ppermute(value, AXES, pairs(move))]
    all_gather x8 -> x0, blocking collectives: 87.6 us -> none  [the longest x2 25.7 us: local(): lax.all_gather(w_query[layer_index], 'fsdp', axis=0, tiled=True)]
  transfers between devices with their start and end apart: 29 -> 90, of which waited for: 25 -> 44; matrix products, arithmetic and copies ran while one was open for 16% -> 11% of each run, Pallas kernels for 0% -> 14%
where the time goes in v1:
time: 591 us; the launch traced here: 582 us
  waiting for transfers between devices  241 us (41%)
  Pallas kernels  129 us (22%)
  starting transfers between devices  100 us (17%)
  local copies, waits for them, and re-layouts  54.4 us (9%)
  other arithmetic  42.6 us (7%)
  between operations  15.3 us (3%)
    ppermute x89, waiting for transfers between devices, send(): return lax.ppermute(value, AXES, pairs(move))  241 us
    pallas_call x11, Pallas kernels, call(): pl.pallas_call(body, out_shape=[jax.ShapeDtypeStruct(s, d) for s, d in ou...  129 us
    ppermute x89, starting transfers between devices, send(): return lax.ppermute(value, AXES, pairs(move))  100 us
    unnamed x104, local copies, waits for them, and re-layouts  19.3 us
    another operation x11, other arithmetic, local(): stacked = [jnp.stack([results[0][i], results[1][i]]) for i in range(9)]  12.5 us
  transfers between devices with their start and end apart: 90, of which 44 were waited for; matrix products, arithmetic and copies ran while one was open for 11% of the time, Pallas kernels for 14%

profile of v1, /device:TPU:1, one launch (start us, length us, event | category | flops | bytes accessed | tf_op | source)
XLA Modules:
  0.0 582.0 jit_solution(672089581173288830)
XLA Ops:
  21.8 6.8 %collective-permute-done.1.p2 = bf16[144,1024]{1,0:T(8,128)(2,1)S(1)} collective-permute-done((bf16[144,1024]{1,0:T(8,128)(2,1)S(1)}, bf16[144,1024]{1,0:T(8,128)(2,1)S(1)}, u32[]{:S(2)}, u32[]{:S(2)}) %collective-permute-start.1) | collective-permute-done | bytes 294944 | tf_op jit(solution)/shard_map/ppermute | solution.py:58
  71.3 26.3 %collective-permute-done.12.r_3_.w3 = bf16[576,576]{1,0:T(8,128)(2,1)} collective-permute-done((bf16[576,576]{1,0:T(8,128)(2,1)S(1)}, bf16[576,576]{1,0:T(8,128)(2,1)}, u32[]{:S(2)}, u32[]{:S(2)}) %collective-permute-start.12) | collective-permute-done | bytes 663584 | tf_op jit(solution)/shard_map/ppermute | solution.py:58
  98.6 13.7 %collective-permute-done.11.r_2_.w2 = bf16[576,576]{1,0:T(8,128)(2,1)} collective-permute-done((bf16[576,576]{1,0:T(8,128)(2,1)S(1)}, bf16[576,576]{1,0:T(8,128)(2,1)}, u32[]{:S(2)}, u32[]{:S(2)}) %collective-permute-start.11) | collective-permute-done | bytes 663584 | tf_op jit(solution)/shard_map/ppermute | solution.py:58
  113.9 19.3 %attend.2 = (bf16[4096,192]{1,0:T(8,128)(2,1)}, bf16[4096,192]{1,0:T(8,128)(2,1)}, f32[2,192,576]{2,1,0:T(8,128)}, f32[2,8,576]{2,1,0:T(8,128)}, bf16[128,576]{1,0:T(8,128)(2,1)}) custom-call(s32[64]{0:T(128)} %reshape.257.tab, s32[2]{0:T(128)} %get-tuple-element.141.own_pos, bf16[128,576]{1,0:T(8,128)(2,1)} %get-tuple-element.59.q, ...), custom_call_target="tpu_custom_call" | custom-call | flops 13200000000 | bytes 1000000 | tf_op jit(solution)/shard_map/attend/pallas_call | solution.py:120
  139.5 7.8 %middle_first.1 = (f32[128,576]{1,0:T(8,128)}, bf16[128,576]{1,0:T(8,128)(2,1)}, f32[128,576]{1,0:T(8,128)}, bf16[128,576]{1,0:T(8,128)(2,1)}, bf16[128,576]{1,0:T(8,128)(2,1)}, /*index=5*/bf16[128,384]{1,0:T(8,128)(2,1)}) custom-call(bf16[128,576]{1,0:T(8,128)(2,1)} %bitcast.156, bf16[128,576]{1,0:T(8,128)(2,1)} %get-tuple-element.61.a.att, ...), custom_call_target="tpu_custom_call" | custom-call | flops 8800000000 | bytes 1000000 | tf_op jit(solution)/shard_map/middle_first/pallas_call | solution.py:120
  180.9 14.3 %collective-permute-done.26.r_3_.w3 = bf16[576,576]{1,0:T(8,128)(2,1)S(1)} collective-permute-done((bf16[576,576]{1,0:T(8,128)(2,1)S(1)}, bf16[576,576]{1,0:T(8,128)(2,1)S(1)}, u32[]{:S(2)}, u32[]{:S(2)}) %collective-permute-start.26) | collective-permute-done | bytes 663584 | tf_op jit(solution)/shard_map/ppermute | solution.py:58
  196.4 13.5 %collective-permute-done.25.r_2_.w2 = bf16[576,576]{1,0:T(8,128)(2,1)S(1)} collective-permute-done((bf16[576,576]{1,0:T(8,128)(2,1)S(1)}, bf16[576,576]{1,0:T(8,128)(2,1)S(1)}, u32[]{:S(2)}, u32[]{:S(2)}) %collective-permute-start.25) | collective-permute-done | bytes 663584 | tf_op jit(solution)/shard_map/ppermute | solution.py:58
  211.9 19.4 %attend.3 = (bf16[4096,192]{1,0:T(8,128)(2,1)}, bf16[4096,192]{1,0:T(8,128)(2,1)}, f32[2,192,576]{2,1,0:T(8,128)}, f32[2,8,576]{2,1,0:T(8,128)}, bf16[128,576]{1,0:T(8,128)(2,1)}) custom-call(s32[64]{0:T(128)} %reshape.257.tab, s32[2]{0:T(128)} %get-tuple-element.141.own_pos, bf16[128,576]{1,0:T(8,128)(2,1)} %get-tuple-element.64.q, ...), custom_call_target="tpu_custom_call" | custom-call | flops 13200000000 | bytes 1000000 | tf_op jit(solution)/shard_map/attend/pallas_call | solution.py:120
  232.6 6.9 %middle_last.1 = (f32[128,576]{1,0:T(8,128)}, bf16[128,576]{1,0:T(8,128)(2,1)}, f32[128,576]{1,0:T(8,128)}) custom-call(f32[128,576]{1,0:T(8,128)} %get-tuple-element.63.s.stream, bf16[128,576]{1,0:T(8,128)(2,1)} %get-tuple-element.66.a.att, bf16[576,576]{1,0:T(8,128)(2,1)} %get-tuple-element.152.o.wo, f32[8,576]{1,0:T(8,128)} %get-tuple-element.62.g.gains, ...), custom_call_target="tpu_custom_call" | custom-call | flops 6600000000 | bytes 1000000 | tf_op jit(solution)/shard_map/middle_last/pallas_call | solution.py:120
  239.5 11.4 %ffn_back.2 = (bf16[4,576,576]{2,1,0:T(8,128)(2,1)}, bf16[4,576,576]{2,1,0:T(8,128)(2,1)}, f32[128,576]{1,0:T(8,128)}, bf16[128,576]{1,0:T(8,128)(2,1)}, bf16[576,576]{1,0:T(8,128)(2,1)}, /*index=5*/f32[8,576]{1,0:T(8,128)}) custom-call(f32[128,576]{1,0:T(8,128)} %bitcast.154, f32[128,576]{1,0:T(8,128)} %get-tuple-element.68.middle, ...), custom_call_target="tpu_custom_call" | custom-call | flops 11000000512 | bytes 1000000 | tf_op jit(solution)/shard_map/ffn_back/pallas_call | solution.py:120
  250.9 20.5 %attend_back.2 = (bf16[2048,384]{1,0:T(8,128)(2,1)}, bf16[2048,384]{1,0:T(8,128)(2,1)}, bf16[128,576]{1,0:T(8,128)(2,1)}) custom-call(s32[64]{0:T(128)} %reshape.257.tab, s32[2]{0:T(128)} %get-tuple-element.141.own_pos, bf16[128,576]{1,0:T(8,128)(2,1)} %get-tuple-element.64.q, bf16[128,576]{1,0:T(8,128)(2,1)} %get-tuple-element.70.d_out, ...), custom_call_target="tpu_custom_call" | custom-call | flops 22000001024 | bytes 1000000 | tf_op jit(solution)/shard_map/attend_back/pallas_call | solution.py:120
  278.9 5.5 collective-permute-done.32
  307.2 11.4 %ffn_back.3 = (bf16[4,576,576]{2,1,0:T(8,128)(2,1)}, bf16[4,576,576]{2,1,0:T(8,128)(2,1)}, f32[128,576]{1,0:T(8,128)}, bf16[128,576]{1,0:T(8,128)(2,1)}, bf16[576,576]{1,0:T(8,128)(2,1)}, /*index=5*/f32[8,576]{1,0:T(8,128)}) custom-call(f32[128,576]{1,0:T(8,128)} %get-tuple-element.82.grad, f32[128,576]{1,0:T(8,128)} %get-tuple-element.83.middle, ...), custom_call_target="tpu_custom_call" | custom-call | flops 11000000512 | bytes 1000000 | tf_op jit(solution)/shard_map/ffn_back/pallas_call | solution.py:120
  318.6 20.7 %attend_back.3 = (bf16[2048,384]{1,0:T(8,128)(2,1)}, bf16[2048,384]{1,0:T(8,128)(2,1)}, bf16[128,576]{1,0:T(8,128)(2,1)}) custom-call(s32[64]{0:T(128)} %reshape.257.tab, s32[2]{0:T(128)} %get-tuple-element.141.own_pos, bf16[128,576]{1,0:T(8,128)(2,1)} %get-tuple-element.59.q, bf16[128,576]{1,0:T(8,128)(2,1)} %get-tuple-element.85.d_out, ...), custom_call_target="tpu_custom_call" | custom-call | flops 22000001024 | bytes 1000000 | tf_op jit(solution)/shard_map/attend_back/pallas_call | solution.py:120
  350.3 6.5 %collective-permute-done.58 = bf16[160,768]{1,0:T(8,128)(2,1)} collective-permute-done((bf16[160,768]{1,0:T(8,128)(2,1)}, bf16[160,768]{1,0:T(8,128)(2,1)}, u32[]{:S(2)}, u32[]{:S(2)}) %collective-permute-start.58) | collective-permute-done | bytes 245792 | tf_op jit(solution)/shard_map/ppermute | solution.py:58
  367.4 5.7 collective-permute-done.61
  378.1 6.1 %collective-permute-done.40 = bf16[512,384]{1,0:T(8,128)(2,1)S(1)} collective-permute-done((bf16[512,384]{1,0:T(8,128)(2,1)S(1)}, bf16[512,384]{1,0:T(8,128)(2,1)S(1)}, u32[]{:S(2)}, u32[]{:S(2)}) %collective-permute-start.40) | collective-permute-done | bytes 393248 | tf_op jit(solution)/shard_map/ppermute | solution.py:58
  390.8 16.8 %collective-permute-done.80 = bf16[576,576]{1,0:T(8,128)(2,1)S(1)} collective-permute-done((bf16[576,576]{1,0:T(8,128)(2,1)S(1)}, bf16[576,576]{1,0:T(8,128)(2,1)S(1)}, u32[]{:S(2)}, u32[]{:S(2)}) %collective-permute-start.80) | collective-permute-done | bytes 663584 | tf_op jit(solution)/shard_map/ppermute | solution.py:58
  414.0 15.2 %collective-permute-done.43.t2 = bf16[128,384]{1,0:T(8,128)(2,1)S(1)} collective-permute-done((bf16[128,384]{1,0:T(8,128)(2,1)S(1)}, bf16[128,384]{1,0:T(8,128)(2,1)S(1)}, u32[]{:S(2)}, u32[]{:S(2)}) %collective-permute-start.43) | collective-permute-done | bytes 98336 | tf_op jit(solution)/shard_map/ppermute | solution.py:58
  448.1 10.2 %collective-permute-done.46 = bf16[160,768]{1,0:T(8,128)(2,1)S(1)} collective-permute-done((bf16[160,768]{1,0:T(8,128)(2,1)S(1)}, bf16[160,768]{1,0:T(8,128)(2,1)S(1)}, u32[]{:S(2)}, u32[]{:S(2)}) %collective-permute-start.46) | collective-permute-done | bytes 245792 | tf_op jit(solution)/shard_map/ppermute | solution.py:58
  460.9 6.8 %collective-permute-done.47 = bf16[160,768]{1,0:T(8,128)(2,1)S(1)} collective-permute-done((bf16[160,768]{1,0:T(8,128)(2,1)S(1)}, bf16[160,768]{1,0:T(8,128)(2,1)S(1)}, u32[]{:S(2)}, u32[]{:S(2)}) %collective-permute-start.47) | collective-permute-done | bytes 245792 | tf_op jit(solution)/shard_map/ppermute | solution.py:58
  488.9 17.2 %collective-permute-done.69 = bf16[576,576]{1,0:T(8,128)(2,1)} collective-permute-done((bf16[576,576]{1,0:T(8,128)(2,1)}, bf16[576,576]{1,0:T(8,128)(2,1)}, u32[]{:S(2)}, u32[]{:S(2)}) %collective-permute-start.69) | collective-permute-done | bytes 663584 | tf_op jit(solution)/shard_map/ppermute | solution.py:58
  537.6 8.6 %collective-permute-done.76 = bf16[576,576]{1,0:T(8,128)(2,1)S(1)} collective-permute-done((bf16[576,576]{1,0:T(8,128)(2,1)S(1)}, bf16[576,576]{1,0:T(8,128)(2,1)S(1)}, u32[]{:S(2)}, u32[]{:S(2)}) %collective-permute-start.76) | collective-permute-done | bytes 663584 | tf_op jit(solution)/shard_map/ppermute | solution.py:58
  546.3 6.6 %collective-permute-done.75 = bf16[576,576]{1,0:T(8,128)(2,1)S(1)} collective-permute-done((bf16[576,576]{1,0:T(8,128)(2,1)S(1)}, bf16[576,576]{1,0:T(8,128)(2,1)S(1)}, u32[]{:S(2)}, u32[]{:S(2)}) %collective-permute-start.75) | collective-permute-done | bytes 663584 | tf_op jit(solution)/shard_map/ppermute | solution.py:58
  (384 shorter events, 269.6 us)
Async XLA Ops:
  7.2 125.9 %all-gather.2.cloned.1.call-start = ((), (), s32[]{:S(2)}) async-start(), calls=%async_computation | async-start | bytes 3133440 | tf_op jit(solution)/shard_map/all_gather | solution.py:396
  58.4 55.5 %collective-permute-start.9 = (bf16[2048,384]{1,0:T(8,128)(2,1)}, bf16[2048,384]{1,0:T(8,128)(2,1)}, u32[]{:S(2)}, u32[]{:S(2)}) collective-permute-start(bf16[2048,384]{1,0:T(8,128)(2,1)} %constant_dynamic-update-slice_fusion.4.kvo), channel_id=1, source_target_pairs={{0,4},{1,5},{2,6},{3,7},{4,0},{5,1},{6,2},{7,3},{8,12},{9,13},{10,... | collective-permute-start | bytes 4718600 | tf_op jit(solution)/shard_map/ppermute | solution.py:58
  64.3 74.3 %collective-permute-start.13 = (bf16[576,576]{1,0:T(8,128)(2,1)S(1)}, bf16[576,576]{1,0:T(8,128)(2,1)S(1)}, u32[]{:S(2)}, u32[]{:S(2)}) collective-permute-start(bf16[576,576]{1,0:T(8,128)(2,1)S(1)} %pad_maximum_fusion.3.r_0_.w0), channel_id=1, source_target_pairs={{0,4},{1,5},{2,6},{3,7},{4,0},{5,1},{6,2},{7,3},{8,12},{9,13},{10,... | collective-permute-start | bytes 1990664 | tf_op jit(solution)/shard_map/ppermute | solution.py:58
  64.4 33.2 %collective-permute-start.12 = (bf16[576,576]{1,0:T(8,128)(2,1)S(1)}, bf16[576,576]{1,0:T(8,128)(2,1)}, u32[]{:S(2)}, u32[]{:S(2)}) collective-permute-start(bf16[576,576]{1,0:T(8,128)(2,1)S(1)} %pad_maximum_fusion.3.r_0_.w0), channel_id=1, source_target_pairs={{0,2},{1,3},{2,0},{3,1},{4,6},{5,7},{6,4},{7,5},{8,10},{9,11},{10,... | collective-permute-start | bytes 1990664 | tf_op jit(solution)/shard_map/ppermute | solution.py:58
  67.0 45.3 %collective-permute-start.11 = (bf16[576,576]{1,0:T(8,128)(2,1)S(1)}, bf16[576,576]{1,0:T(8,128)(2,1)}, u32[]{:S(2)}, u32[]{:S(2)}) collective-permute-start(bf16[576,576]{1,0:T(8,128)(2,1)S(1)} %pad_maximum_fusion.3.r_0_.w0), channel_id=1, source_target_pairs={{0,3},{1,0},{2,1},{3,2},{4,7},{5,4},{6,5},{7,6},{8,11},{9,8},{10,9... | collective-permute-start | bytes 1990664 | tf_op jit(solution)/shard_map/ppermute | solution.py:58
  68.0 45.2 %collective-permute-start.10 = (bf16[576,576]{1,0:T(8,128)(2,1)S(1)}, bf16[576,576]{1,0:T(8,128)(2,1)}, u32[]{:S(2)}, u32[]{:S(2)}) collective-permute-start(bf16[576,576]{1,0:T(8,128)(2,1)S(1)} %pad_maximum_fusion.3.r_0_.w0), channel_id=1, source_target_pairs={{0,1},{1,2},{2,3},{3,0},{4,5},{5,6},{6,7},{7,4},{8,9},{9,10},{10,1... | collective-permute-start | bytes 1990664 | tf_op jit(solution)/shard_map/ppermute | solution.py:58
  97.7 41.0 %collective-permute-start.16 = (bf16[576,576]{1,0:T(8,128)(2,1)}, bf16[576,576]{1,0:T(8,128)(2,1)}, u32[]{:S(2)}, u32[]{:S(2)}) collective-permute-start(bf16[576,576]{1,0:T(8,128)(2,1)} %collective-permute-done.12.r_3_.w3), channel_id=1, source_target_pairs={{0,4},{1,5},{2,6},{3,7},{4,0},{5,1},{6,2},{7,3},{8,12},{9,13},{10,... | collective-permute-start | bytes 1990664 | tf_op jit(solution)/shard_map/ppermute | solution.py:58
  171.9 40.0 %collective-permute-start.23 = (bf16[2048,384]{1,0:T(8,128)(2,1)}, bf16[2048,384]{1,0:T(8,128)(2,1)}, u32[]{:S(2)}, u32[]{:S(2)}) collective-permute-start(bf16[2048,384]{1,0:T(8,128)(2,1)} %constant_dynamic-update-slice_fusion.15.kvo), channel_id=1, source_target_pairs={{0,4},{1,5},{2,6},{3,7},{4,0},{5,1},{6,2},{7,3},{8,12},{9,13},{10,... | collective-permute-start | bytes 4718600 | tf_op jit(solution)/shard_map/ppermute | solution.py:58
  177.6 32.3 %collective-permute-start.25 = (bf16[576,576]{1,0:T(8,128)(2,1)S(1)}, bf16[576,576]{1,0:T(8,128)(2,1)S(1)}, u32[]{:S(2)}, u32[]{:S(2)}) collective-permute-start(bf16[576,576]{1,0:T(8,128)(2,1)S(1)} %pad_maximum_fusion.4.r_0_.w0), channel_id=1, source_target_pairs={{0,3},{1,0},{2,1},{3,2},{4,7},{5,4},{6,5},{7,6},{8,11},{9,8},{10,9... | collective-permute-start | bytes 1990664 | tf_op jit(solution)/shard_map/ppermute | solution.py:58
  178.8 32.6 %collective-permute-start.24 = (bf16[576,576]{1,0:T(8,128)(2,1)S(1)}, bf16[576,576]{1,0:T(8,128)(2,1)}, u32[]{:S(2)}, u32[]{:S(2)}) collective-permute-start(bf16[576,576]{1,0:T(8,128)(2,1)S(1)} %pad_maximum_fusion.4.r_0_.w0), channel_id=1, source_target_pairs={{0,1},{1,2},{2,3},{3,0},{4,5},{5,6},{6,7},{7,4},{8,9},{9,10},{10,1... | collective-permute-start | bytes 1990664 | tf_op jit(solution)/shard_map/ppermute | solution.py:58
  179.1 52.1 %collective-permute-start.27 = (bf16[576,576]{1,0:T(8,128)(2,1)S(1)}, bf16[576,576]{1,0:T(8,128)(2,1)}, u32[]{:S(2)}, u32[]{:S(2)}) collective-permute-start(bf16[576,576]{1,0:T(8,128)(2,1)S(1)} %pad_maximum_fusion.4.r_0_.w0), channel_id=1, source_target_pairs={{0,4},{1,5},{2,6},{3,7},{4,0},{5,1},{6,2},{7,3},{8,12},{9,13},{10,... | collective-permute-start | bytes 1990664 | tf_op jit(solution)/shard_map/ppermute | solution.py:58
  195.2 36.0 %collective-permute-start.30 = (bf16[576,576]{1,0:T(8,128)(2,1)S(1)}, bf16[576,576]{1,0:T(8,128)(2,1)S(1)}, u32[]{:S(2)}, u32[]{:S(2)}) collective-permute-start(bf16[576,576]{1,0:T(8,128)(2,1)S(1)} %collective-permute-done.26.r_3_.w3), channel_id=1, source_target_pairs={{0,4},{1,5},{2,6},{3,7},{4,0},{5,1},{6,2},{7,3},{8,12},{9,13},{10,... | collective-permute-start | bytes 1990664 | tf_op jit(solution)/shard_map/ppermute | solution.py:58
  294.3 68.1 %collective-permute-start.78 = (bf16[4,576,576]{2,1,0:T(8,128)(2,1)}, bf16[4,576,576]{2,1,0:T(8,128)(2,1)}, u32[]{:S(2)}, u32[]{:S(2)}) collective-permute-start(bf16[4,576,576]{2,1,0:T(8,128)(2,1)} %get-tuple-element.106), channel_id=1, source_target_pairs={{0,4},{1,5},{2,6},{3,7},{4,0},{5,1},{6,2},{7,3},{8,12},{9,13},{10,... | collective-permute-start | bytes 7962632 | tf_op jit(solution)/shard_map/ppermute | solution.py:58
  303.6 35.7 %collective-permute-start.56 = (bf16[4,160,768]{2,1,0:T(8,128)(2,1)}, bf16[4,160,768]{2,1,0:T(8,128)(2,1)S(1)}, u32[]{:S(2)}, u32[]{:S(2)}) collective-permute-start(bf16[4,160,768]{2,1,0:T(8,128)(2,1)} %get-tuple-element.102), channel_id=1, source_target_pairs={{0,4},{1,5},{2,6},{3,7},{4,0},{5,1},{6,2},{7,3},{8,12},{9,13},{10,... | collective-permute-start | bytes 2949128 | tf_op jit(solution)/shard_map/ppermute | solution.py:58
  374.1 33.6 %collective-permute-start.80 = (bf16[576,576]{1,0:T(8,128)(2,1)S(1)}, bf16[576,576]{1,0:T(8,128)(2,1)S(1)}, u32[]{:S(2)}, u32[]{:S(2)}) collective-permute-start(bf16[576,576]{1,0:T(8,128)(2,1)S(1)} %get-tuple-element.151), channel_id=1, source_target_pairs={{0,1},{1,2},{2,3},{3,0},{4,5},{5,6},{6,7},{7,4},{8,9},{9,10},{10,1... | collective-permute-start | bytes 1990664 | tf_op jit(solution)/shard_map/ppermute | solution.py:58
  377.3 32.2 %collective-permute-start.65 = (bf16[160,768]{1,0:T(8,128)(2,1)S(1)}, bf16[160,768]{1,0:T(8,128)(2,1)S(1)}, u32[]{:S(2)}, u32[]{:S(2)}) collective-permute-start(bf16[160,768]{1,0:T(8,128)(2,1)S(1)} %add_convert_fusion.13), channel_id=1, source_target_pairs={{0,64},{1,65},{2,66},{3,67},{4,20},{5,21},{6,22},{7,23},{8,72},{9,... | collective-permute-start | bytes 737288 | tf_op jit(solution)/shard_map/ppermute | solution.py:58
  408.0 29.3 %collective-permute-start.84 = (bf16[576,576]{1,0:T(8,128)(2,1)S(1)}, bf16[576,576]{1,0:T(8,128)(2,1)S(1)}, u32[]{:S(2)}, u32[]{:S(2)}) collective-permute-start(bf16[576,576]{1,0:T(8,128)(2,1)S(1)} %fusion.3), channel_id=1, source_target_pairs={{0,16},{1,17},{2,18},{3,19},{4,68},{5,69},{6,70},{7,71},{8,24},{9,... | collective-permute-start | bytes 1990664 | tf_op jit(solution)/shard_map/ppermute | solution.py:58
  409.5 28.0 %collective-permute-start.83 = (bf16[576,576]{1,0:T(8,128)(2,1)S(1)}, bf16[576,576]{1,0:T(8,128)(2,1)S(1)}, u32[]{:S(2)}, u32[]{:S(2)}) collective-permute-start(bf16[576,576]{1,0:T(8,128)(2,1)S(1)} %fusion.3), channel_id=1, source_target_pairs={{0,24},{1,25},{2,26},{3,27},{4,100},{5,101},{6,102},{7,103},{8,0},... | collective-permute-start | bytes 1990664 | tf_op jit(solution)/shard_map/ppermute | solution.py:58
  437.9 32.6 %collective-permute-start.87 = (bf16[576,576]{1,0:T(8,128)(2,1)S(1)}, bf16[576,576]{1,0:T(8,128)(2,1)S(1)}, u32[]{:S(2)}, u32[]{:S(2)}) collective-permute-start(bf16[576,576]{1,0:T(8,128)(2,1)S(1)} %add_convert_fusion.7), channel_id=1, source_target_pairs={{0,64},{1,65},{2,66},{3,67},{4,20},{5,21},{6,22},{7,23},{8,72},{9,... | collective-permute-start | bytes 1990664 | tf_op jit(solution)/shard_map/ppermute | solution.py:58
  438.5 32.1 %collective-permute-start.86 = (bf16[576,576]{1,0:T(8,128)(2,1)S(1)}, bf16[576,576]{1,0:T(8,128)(2,1)S(1)}, u32[]{:S(2)}, u32[]{:S(2)}) collective-permute-start(bf16[576,576]{1,0:T(8,128)(2,1)S(1)} %add_convert_fusion.7), channel_id=1, source_target_pairs={{0,96},{1,97},{2,98},{3,99},{4,28},{5,29},{6,30},{7,31},{8,104},{9... | collective-permute-start | bytes 1990664 | tf_op jit(solution)/shard_map/ppermute | solution.py:58
  439.4 31.7 %collective-permute-start.85 = (bf16[576,576]{1,0:T(8,128)(2,1)S(1)}, bf16[576,576]{1,0:T(8,128)(2,1)S(1)}, u32[]{:S(2)}, u32[]{:S(2)}) collective-permute-start(bf16[576,576]{1,0:T(8,128)(2,1)S(1)} %add_convert_fusion.7), channel_id=1, source_target_pairs={{0,32},{1,33},{2,34},{3,35},{4,12},{5,13},{6,14},{7,15},{8,40},{9,... | collective-permute-start | bytes 1990664 | tf_op jit(solution)/shard_map/ppermute | solution.py:58
  470.5 35.6 %collective-permute-start.69 = (bf16[576,576]{1,0:T(8,128)(2,1)}, bf16[576,576]{1,0:T(8,128)(2,1)}, u32[]{:S(2)}, u32[]{:S(2)}) collective-permute-start(bf16[576,576]{1,0:T(8,128)(2,1)} %get-tuple-element.148), channel_id=1, source_target_pairs={{0,1},{1,2},{2,3},{3,0},{4,5},{5,6},{6,7},{7,4},{8,9},{9,10},{10,1... | collective-permute-start | bytes 1990664 | tf_op jit(solution)/shard_map/ppermute | solution.py:58
  477.2 35.3 %collective-permute-start.88 = (bf16[576,576]{1,0:T(8,128)(2,1)}, bf16[576,576]{1,0:T(8,128)(2,1)}, u32[]{:S(2)}, u32[]{:S(2)}) collective-permute-start(bf16[576,576]{1,0:T(8,128)(2,1)} %add_convert_fusion.6), channel_id=1, source_target_pairs={{0,4},{1,5},{2,6},{3,7},{4,0},{5,1},{6,2},{7,3},{8,12},{9,13},{10,... | collective-permute-start | bytes 1990664 | tf_op jit(solution)/shard_map/ppermute | solution.py:58
  483.4 30.3 %collective-permute-start.54 = (bf16[160,768]{1,0:T(8,128)(2,1)}, bf16[160,768]{1,0:T(8,128)(2,1)S(1)}, u32[]{:S(2)}, u32[]{:S(2)}) collective-permute-start(bf16[160,768]{1,0:T(8,128)(2,1)} %add_convert_fusion.15), channel_id=1, source_target_pairs={{0,64},{1,65},{2,66},{3,67},{4,20},{5,21},{6,22},{7,23},{8,72},{9,... | collective-permute-start | bytes 737288 | tf_op jit(solution)/shard_map/ppermute | solution.py:58
  (111 other events, 1306.0 us)
Sparse Core Ops, SparseCore 0:
  46.5 61.9 all-gather.1

commit v2 on v1

--- a/solution.py
+++ b/solution.py
@@ -24,6 +24,7 @@
 BF = jnp.bfloat16
 AXES = ("ctx", "fsdp")
 OFFS = (0, -1, 1, 2)
+PACK = 2 * D + 2 * 224
 
 
 def nn(a, b):
@@ -88,30 +89,42 @@
     ]
 
 
+def after(value, *others):
+    return lax.optimization_barrier((value, *others))[0]
+
+
 def total(parts):
     return sum(p.astype(F32) for p in parts)
 
 
+def plane_one(k):
+    return plane(0, k)
+
+
+def plane_two(k):
+    return plane(1, k)
+
+
+def swap(values):
+    return [send(v, other_core) for v in values]
+
+
 def gather_plane(value):
-    first = jnp.concatenate(gather_stage(value, lambda k: plane(0, k)), 0)
-    own = jnp.concatenate(gather_stage(first, lambda k: plane(1, k)), 0)
-    return own, send(own, other_core)
-
-
-def scatter_plane(own, other):
+    first = jnp.concatenate(gather_stage(value, plane_one), 0)
+    own = gather_stage(first, plane_two)
+    return own + swap(own), first
+
+
+def scatter_plane(own, other, waits=()):
     both = total([own, send(other, other_core)]).astype(BF)
     parts = both.reshape((4, 512) + own.shape[1:])
-    one = total(scatter_stage([parts[j] for j in range(4)], lambda k: plane(1, k))).astype(BF)
-    one = one.reshape((4, 128) + own.shape[1:])
-    return scatter_stage([one[j] for j in range(4)], lambda k: plane(0, k))
-
-
-def reduce_all(own, other):
-    half = total([own, send(other, other_core)]).astype(BF)
-    part = total(scatter_stage([half[j] for j in range(4)], along_x)).astype(BF)
-    part = total(gather_stage(part, lambda k: plane(0, k))).astype(BF)
-    part = total(gather_stage(part, lambda k: plane(1, k))).astype(BF)
-    return part, send(part, other_core)
+    one = total(scatter_stage([parts[j] for j in range(4)], plane_two)).astype(BF)
+    one = after(one, *waits).reshape((4, 128) + own.shape[1:])
+    return scatter_stage([one[j] for j in range(4)], plane_one)
+
+
+def add_cores(own, other):
+    return total([own, send(other, other_core)]).astype(BF)
 
 
 def call(body, outs, args, smem=0, scratch=(), us=5.0, name=None):
@@ -193,16 +206,18 @@
     return key <= query
 
 
-def attend_kernel(tab, own_pos, q, kvo, kvt, kp, vp, ot, lse, att, qbd, acc, stat):
+def attend_kernel(tab, own_pos, q, *rest):
+    kv, (kp, vp, ot, lse, att, qbd, acc, stat) = rest[:8], rest[8:]
+
     def place(s, carry):
-        for base, ref in ((0, kvo), (32, kvt)):
-            at = pl.ds(pl.multiple_of(tab[base + s] * BLK, BLK), BLK)
+        for j, ref in enumerate(kv):
+            at = pl.ds(pl.multiple_of(tab[8 * j + s] * BLK, BLK), BLK)
             rows = ref[pl.ds(pl.multiple_of(s * BLK, BLK), BLK), :]
             kp[at, :] = rows[:, :KW]
             vp[at, :] = rows[:, KW:]
         return carry
 
-    lax.fori_loop(0, 32, place, 0)
+    lax.fori_loop(0, 8, place, 0)
     for block in range(2):
         position = own_pos[block]
         spread(q, qbd, block)
@@ -243,43 +258,61 @@
 
 def ffn_forward(n2, pieces):
     out = None
-    for p in pieces:
-        gate = nt(n2, p[0:KW, :])
-        up = nt(n2, p[KW : 2 * KW, :])
-        hidden = (gate * jax.nn.sigmoid(gate) * up).astype(BF)
-        term = nn(hidden, p[2 * KW : 3 * KW, :])
-        out = term if out is None else out + term
+    for ref in pieces:
+        for k in range(4):
+            gate = nt(n2, ref[k, 0:KW, :])
+            up = nt(n2, ref[k, KW : 2 * KW, :])
+            hidden = (gate * jax.nn.sigmoid(gate) * up).astype(BF)
+            term = nn(hidden, ref[k, 2 * KW : 3 * KW, :])
+            out = term if out is None else out + term
     return out
 
 
-def middle_kernel(stream, att, wo, gains, gain_row, w0, w1, w2, w3, v0, v1, v2, v3, *rest):
-    if len(rest) > 3:
-        wqkv, cos, sin, middle_ref, n2_ref, out, normed, q, kv = rest
-    else:
-        middle_ref, n2_ref, out = rest
-    middle = stream[...].astype(F32) + nn(att[...], wo[...])
+def middle_first_kernel(
+    place, stream, att, gains, w, v, r0, r1, r2, r3, s0, s1, s2, s3, cos, sin,
+    middle_ref, n2_ref, out, normed, q, kv, wo0, wqkv1, wo1,
+):
+    x, c = place[0], place[1]
+
+    def sort(outs, projections):
+        for j in range(4):
+            owner = lax.rem(x + (OFFS[j] + 4), 4)
+            at = pl.ds(pl.multiple_of(owner * 144, 16), 144)
+            wo0[at, :] = outs[j][:, :D]
+            wo1[at, :] = outs[j][:, D:]
+            wqkv1[at, :] = projections[j][:, :960]
+
+    @pl.when(c == 0)
+    def _():
+        sort((r0, r1, r2, r3), (s0, s1, s2, s3))
+
+    @pl.when(c == 1)
+    def _():
+        sort((s0, s1, s2, s3), (r0, r1, r2, r3))
+
+    middle = stream[...].astype(F32) + nn(att[...], wo0[...])
     middle_ref[...] = middle
-    n2 = (middle * rms(middle) * gains[gain_row + 1 : gain_row + 2, :]).astype(BF)
+    n2 = (middle * rms(middle) * gains[1:2, :]).astype(BF)
     n2_ref[...] = n2
-    result = middle + ffn_forward(n2, (w0, w1, w2, w3, v0, v1, v2, v3))
+    result = middle + ffn_forward(n2, (w, v))
     out[...] = result
-    if len(rest) > 3:
-        n = (result * rms(result) * gains[gain_row + 2 : gain_row + 3, :]).astype(BF)
-        normed[...] = n
-        project(n, wqkv[...], cos[...], sin[...], q, kv)
-
-
-def ffn_back_kernel(
-    gain_row, grad, middle, n2_ref, att, wo, gains, w0, w1, w2, w3, v0, v1, v2, v3,
-    g_own, g_oth, mid_grad, d_out, d_wo, d_gain,
-):
-    g = grad[...]
-    branch = g.astype(BF)
-    n2 = n2_ref[...]
+    n = (result * rms(result) * gains[2:3, :]).astype(BF)
+    normed[...] = n
+    project(n, wqkv1[...], cos[...], sin[...], q, kv)
+
+
+def middle_last_kernel(stream, att, wo, gains, w, v, middle_ref, n2_ref, out):
+    middle = stream[...] + nn(att[...], wo[...])
+    middle_ref[...] = middle
+    n2 = (middle * rms(middle) * gains[3:4, :]).astype(BF)
+    n2_ref[...] = n2
+    out[...] = (middle + ffn_forward(n2, (w, v))).T
+
+
+def ffn_grads(branch, n2, weights, dst):
     n2_grad = None
-    for j, p in enumerate((w0, w1, w2, w3, v0, v1, v2, v3)):
-        dst = g_own if j < 4 else g_oth
-        k = j % 4
+    for k in range(4):
+        p = weights.at[k]
         gate = nt(n2, p[0:KW, :])
         up = nt(n2, p[KW : 2 * KW, :])
         s = jax.nn.sigmoid(gate)
@@ -292,6 +325,18 @@
         dst[k, 2 * KW : 3 * KW, :] = tn(hidden, branch).astype(BF)
         term = nn(gate_grad, p[0:KW, :]) + nn(up_grad, p[KW : 2 * KW, :])
         n2_grad = term if n2_grad is None else n2_grad + term
+    return n2_grad
+
+
+def ffn_back_other_kernel(grad, n2, v, g_oth, part):
+    part[...] = ffn_grads(grad[...].astype(BF), n2[...], v, g_oth)
+
+
+def ffn_back_own_kernel(
+    gain_row, grad, n2, w, half_grad, middle, att, wo, gains, g_own, mid_grad, d_out, d_wo, d_gain
+):
+    g = grad[...]
+    n2_grad = half_grad[...] + ffn_grads(g.astype(BF), n2[...], w, g_own)
     part, gain_grad = norm_back(middle[...], gains[gain_row + 1 : gain_row + 2, :], n2_grad)
     m_grad = g + part
     mid_grad[...] = m_grad
@@ -354,7 +399,7 @@
 
 def project_back_kernel(
     gain_row, place_ref, t0, t1, t2, t3, dq_pre, normed, stream, gains, wqkv, mid_grad,
-    d_wo, d_gain_two, cos, sin, grad, g_own, g_oth, kbuf, full,
+    d_wo, d_gain_two, cos, sin, grad, g_own, g_oth, kbuf, full, side,
 ):
     x, c = place_ref[0], place_ref[1]
     dkv = t0[...].astype(F32) + t1[...].astype(F32) + t2[...].astype(F32) + t3[...].astype(F32)
@@ -364,22 +409,83 @@
     dqk = jnp.concatenate([dq_pre[...], dk_pre], 1)
     dv_pre = dkv[:, KW:].astype(BF)
     n = normed[...]
-    full[0, :D, :] = tn(n, dqk).astype(BF)
-    full[1, :D, :] = jnp.concatenate([tn(n, dv_pre).astype(BF), d_wo[...]], 1)
+    full[0] = tn(n, dq_pre[...]).astype(BF)
+    full[1] = d_wo[...]
+    side[:, : 2 * KW] = tn(n, jnp.concatenate([dk_pre, dv_pre], 1)).astype(BF)
+    side[:, 2 * KW :] = jnp.zeros((D, KW), BF)
     n_grad = nt(jnp.concatenate([dqk, dv_pre], 1), wqkv[...])
     part, gain_grad = norm_back(stream[...].astype(F32), gains[gain_row : gain_row + 1, :], n_grad)
-    grad[...] = mid_grad[...] + part
-    full[0, D:, :] = jnp.zeros((16, 768), BF)
-    full[1, D:, :] = jnp.zeros((16, 768), BF)
-    full[0, D:, :D] = jnp.broadcast_to(gain_grad, (16, D)).astype(BF)
-    full[1, D:, :D] = jnp.broadcast_to(d_gain_two[0:1, :], (16, D)).astype(BF)
+    total_grad = mid_grad[...] + part
+    grad[...] = total_grad.T if grad.shape[0] == D else total_grad
+    row = lax.broadcasted_iota(jnp.int32, (16, D), 0)
+    both_gains = jnp.where(row == 0, gain_grad, d_gain_two[0:1, :]).astype(BF)
+
+    def write(low, high):
+        for j in range(4):
+            start = pl.multiple_of(lax.rem(x + (OFFS[j] + 4), 4) * 144, 16)
+            low[j, :144, :] = full[0, pl.ds(start, 144), :]
+            high[j, :144, :] = full[1, pl.ds(start, 144), :]
+            low[j, 144:, :] = side[pl.ds(start, 80), :]
+            high[j, 144:208, :] = side[pl.ds(start + 80, 64), :]
+            high[j, 208:, :] = both_gains
+
+    @pl.when(c == 0)
+    def _():
+        write(g_own, g_oth)
+
+    @pl.when(c == 1)
+    def _():
+        write(g_oth, g_own)
+
+
+def pack_kernel(place, *refs):
+    outs, tmp = refs[16:20], refs[20]
+    at = 0
+    for k, rows in enumerate((D, D, 224, 224)):
+        shares = refs[4 * k : 4 * k + 4]
+        tmp[at : at + rows, :] = sum(r[...].astype(F32) for r in shares).astype(BF)
+        at += rows
     for j in range(4):
-        owner = lax.rem(x + (OFFS[j] + 4), 4)
-        at = pl.ds(pl.multiple_of(owner * 144, 16), 144)
-        g_own[j, :144, :] = full[c, at, :]
-        g_own[j, 144:, :] = full[c, D:, :]
-        g_oth[j, :144, :] = full[1 - c, at, :]
-        g_oth[j, 144:, :] = full[1 - c, D:, :]
+        start = lax.rem(place[2] + (OFFS[j] + 4), 4) * (PACK // 4)
+        outs[j][...] = tmp[pl.ds(pl.multiple_of(start, 16), PACK // 4), :]
+
+
+def unpack_kernel(
+    place, m0, m1, m2, m3, t0, t1, t2, t3,
+    dq, dk, dv, do, dg, du, dd, gains, mine, theirs, turn,
+):
+    c = place[1]
+    for j in range(4):
+        start = lax.rem(place[2] + (OFFS[j] + 4), 4) * (PACK // 4)
+        mine[pl.ds(pl.multiple_of(start, 16), PACK // 4), :] = (m0, m1, m2, m3)[j][...]
+        start = lax.rem(place[3] + (OFFS[j] + 4), 4) * (PACK // 4)
+        theirs[pl.ds(pl.multiple_of(start, 16), PACK // 4), :] = (t0, t1, t2, t3)[j][...]
+    for layer in range(2):
+        a, b = mine.at[D * layer : D * layer + D], theirs.at[D * layer : D * layer + D]
+        at_a = pl.ds(pl.multiple_of(c * KW, 64), KW)
+        at_b = pl.ds(pl.multiple_of((1 - c) * KW, 64), KW)
+        for k, ref in enumerate((dg, du, dd)):
+            turn[at_a, :] = a[KW * k : KW * k + KW, :].astype(F32)
+            turn[at_b, :] = b[KW * k : KW * k + KW, :].astype(F32)
+            ref[layer] = turn[...].T
+
+    def write(low, high):
+        for layer in range(2):
+            at = 2 * D + 224 * layer
+            dq[layer] = low[at : at + 144, :].astype(F32)
+            do[layer] = high[at : at + 144, :].astype(F32)
+            for ref, lanes in ((dk, slice(0, KW)), (dv, slice(KW, 2 * KW))):
+                ref[layer, :80, :] = low[at + 144 : at + 224, lanes].astype(F32)
+                ref[layer, 80:, :] = high[at + 144 : at + 208, lanes].astype(F32)
+            gains[8 * layer : 8 * layer + 8, :] = high[at + 208 : at + 224, :].astype(F32)[:8, :]
+
+    @pl.when(c == 0)
+    def _():
+        write(mine, theirs)
+
+    @pl.when(c == 1)
+    def _():
+        write(theirs, mine)
 
 
 def local(tokens, pairing, cotangent, w_query, w_key, w_value, w_out, w_gate, w_up, w_down, attn_gain, ffn_gain):
@@ -392,9 +498,9 @@
         [w_query[0], w_key[0], w_value[0], gains_in, jnp.zeros((144, 60), BF)], 1
     )
     first_pieces = gather_stage(bundle, along_x)
-    rest = jnp.concatenate([w_out[0], w_query[1], w_key[1], w_value[1], w_out[1]], 1)
-    rest = lax.all_gather(rest, "fsdp", axis=0, tiled=True)
-    wo = [rest[:, :D], rest[:, D + 960 :]]
+    outs = jnp.concatenate([w_out[0], w_out[1]], 1)
+    later = jnp.concatenate([w_query[1], w_key[1], w_value[1], jnp.zeros((144, KW), BF)], 1)
+    rest = gather_stage(jnp.where(c == 0, outs, later), along_x)
 
     def halves(layer):
         parts = [
@@ -403,10 +509,8 @@
         ]
         return jnp.concatenate(parts, 0)
 
-    ffn = []
-    for layer in range(2):
-        own = gather_stage(halves(layer), along_x)
-        ffn.append(own + [send(p, other_core) for p in own])
+    def gather_ffn(mine):
+        return lax.all_gather(mine, "fsdp", axis=0)
 
     spot = jnp.arange(16, dtype=jnp.int32)
     step = jnp.array(OFFS, jnp.int32)
@@ -426,7 +530,8 @@
     cos1, sin1 = jnp.cos(angle), jnp.sin(angle)
     cos = jnp.concatenate([cos1] * 4, 1)
     sin = jnp.concatenate([-sin1, sin1] * 2, 1)
-    place = jnp.stack([x, c]).astype(jnp.int32)
+    spots = [x, c, jnp.where(c == 0, y, z), jnp.where(c == 0, z, y)]
+    place = jnp.stack(spots).astype(jnp.int32)
 
     act = (ROWS, D)
     stream0 = tokens[0]
@@ -441,7 +546,6 @@
     )
 
     def attend(q, kv):
-        own, oth = gather_plane(kv)
         return call(
             attend_kernel,
             [
@@ -451,48 +555,69 @@
                 ((2, 8, D), F32),
                 (act, BF),
             ],
-            [tab, own_pos, q, own, oth],
+            [tab, own_pos, q, *kv],
             smem=2,
             scratch=[pltpu.VMEM((D, KW), BF), pltpu.VMEM((KW, D), F32), pltpu.VMEM((8, D), F32)],
             us=12.0,
             name="attend",
         )
 
+    ffn0 = gather_ffn(after(halves(0), *first_pieces[1:3]))
+    kv0, first0 = gather_plane(kv0)
+    ffn1 = gather_ffn(after(halves(1), first0))
+    ffn0 = [ffn0, send(after(ffn0, *kv0[:4]), other_core)]
     kp0, vp0, ot0, lse0, att0 = attend(q0, kv0)
-    wqkv1 = rest[:, D : D + 960]
-    middle0, n20, stream1, normed1, q1, kv1 = call(
-        lambda s, a, o, g, *r: middle_kernel(s, a, o, g, 0, *r),
-        [(act, F32), (act, BF), (act, F32), (act, BF), (act, BF), ((ROWS, 384), BF)],
-        [stream0, att0, wo[0], gains, *ffn[0], wqkv1, cos, sin],
+    rest = rest + swap([after(r, att0) for r in rest])
+    middle0, n20, stream1, normed1, q1, kv1, wo0, wqkv1, wo1 = call(
+        middle_first_kernel,
+        [
+            (act, F32),
+            (act, BF),
+            (act, F32),
+            (act, BF),
+            (act, BF),
+            ((ROWS, 384), BF),
+            ((D, D), BF),
+            ((D, 960), BF),
+            ((D, D), BF),
+        ],
+        [place, stream0, att0, gains, *ffn0, *rest, cos, sin],
+        smem=1,
         us=8.0,
         name="middle_first",
     )
+    kv1, _ = gather_plane(kv1)
+    ffn1 = [ffn1, send(after(ffn1, *kv1[:4]), other_core)]
     kp1, vp1, ot1, lse1, att1 = attend(q1, kv1)
     middle1, n21, out = call(
-        lambda s, a, o, g, *r: middle_kernel(s, a, o, g, 2, *r),
-        [(act, F32), (act, BF), (act, F32)],
-        [stream1, att1, wo[1], gains, *ffn[1]],
+        middle_last_kernel,
+        [(act, F32), (act, BF), ((D, ROWS), F32)],
+        [stream1, att1, wo1, gains, *ffn1],
         us=6.0,
         name="middle_last",
     )
 
-    def back(layer, grad, middle, n2, att, q, kp, vp, ot, lse, normed, stream, wqkv):
-        g_own, g_oth, mid_grad, d_out, d_wo, d_gain_two = call(
-            functools.partial(ffn_back_kernel, 2 * layer),
-            [
-                ((4, D, D), BF),
-                ((4, D, D), BF),
-                (act, F32),
-                (act, BF),
-                ((D, D), BF),
-                ((8, D), F32),
-            ],
-            [grad, middle, n2, att, wo[layer], gains, *ffn[layer]],
-            us=10.0,
-            name="ffn_back",
+    def ffn_back(layer, grad, middle, n2, att, wo, ffn, waits=()):
+        g_oth, part = call(
+            ffn_back_other_kernel,
+            [((4, D, D), BF), (act, F32)],
+            [grad, n2, ffn[1]],
+            us=5.0,
+            name="ffn_back_other",
         )
-        ffn_sums = reduce_all(g_own, g_oth)
-        dkv_own, dkv_oth, dq_pre = call(
+        g_oth = send(g_oth, other_core)
+        g_own, mid_grad, d_out, *small = call(
+            functools.partial(ffn_back_own_kernel, 2 * layer),
+            [((4, D, D), BF), (act, F32), (act, BF), ((D, D), BF), ((8, D), F32)],
+            [grad, n2, ffn[0], after(part, *waits), middle, att, wo, gains],
+            us=6.0,
+            name="ffn_back_own",
+        )
+        half = total([g_own, g_oth]).astype(BF)
+        return after(d_out, half), half, mid_grad, small
+
+    def attend_back(q, d_out, kp, vp, ot, lse):
+        return call(
             attend_back_kernel,
             [((2048, 384), BF), ((2048, 384), BF), (act, BF)],
             [tab, own_pos, q, d_out, kp, vp, ot, lse, cos, sin],
@@ -508,51 +633,81 @@
             us=20.0,
             name="attend_back",
         )
-        terms = scatter_plane(dkv_own, dkv_oth)
-        new_grad, a_own, a_oth = call(
+
+    def project_back(layer, terms, dq_pre, normed, stream, wqkv, mid_grad, d_wo, d_gain_two):
+        return call(
             functools.partial(project_back_kernel, 2 * layer),
-            [(act, F32), ((4, 160, 768), BF), ((4, 160, 768), BF)],
+            [((D, ROWS) if layer == 0 else act, F32), ((4, 224, D), BF), ((4, 224, D), BF)],
             [place, *terms, dq_pre, normed, stream, gains, wqkv, mid_grad, d_wo, d_gain_two, cos, sin],
             smem=1,
-            scratch=[pltpu.VMEM((ROWS, 256), F32), pltpu.VMEM((2, D + 16, 768), BF)],
+            scratch=[
+                pltpu.VMEM((ROWS, 256), F32),
+                pltpu.VMEM((2, D, D), BF),
+                pltpu.VMEM((D, D), BF),
+            ],
             us=5.0,
             name="project_back",
         )
-        attn_sums = reduce_all(a_own, a_oth)
-        return new_grad, ffn_sums, attn_sums
-
-    grad1, ffn1, attn1 = back(
-        1, cotangent[0], middle1, n21, att1, q1, kp1, vp1, ot1, lse1, normed1, stream1, wqkv1
-    )
-    grad0, ffn0, attn0 = back(
-        0, grad1, middle0, n20, att0, q0, kp0, vp0, ot0, lse0, normed0, stream0, wqkv0
-    )
-
-    def ordered(sums):
-        mine, theirs = (s.astype(F32) for s in sums)
-        return jnp.where(c == 0, mine, theirs), jnp.where(c == 0, theirs, mine)
-
-    results = []
-    for ffn_sums, attn_sums in ((ffn0, attn0), (ffn1, attn1)):
-        low, high = ordered(ffn_sums)
-        both = jnp.concatenate([low.reshape(3, KW, D), high.reshape(3, KW, D)], 1)
-        one, two = ordered(attn_sums)
-        gain_at = lambda v: lax.dynamic_slice_in_dim(v[144, :D], 144 * x, 144, 0)
-        results.append(
-            (
-                one[:144, :D],
-                one[:144, D:],
-                two[:144, :KW],
-                two[:144, KW:],
-                both[0].T,
-                both[1].T,
-                both[2],
-                gain_at(one),
-                gain_at(two),
-            )
-        )
-    stacked = [jnp.stack([results[0][i], results[1][i]]) for i in range(9)]
-    return (out[None], grad0[None], *stacked)
+
+    def share(half, order):
+        return scatter_stage([half[j] for j in order], along_x)
+
+    owners_x = [(x + k) % 4 for k in OFFS]
+
+    d_out, half, mid_grad, small = ffn_back(1, cotangent[0], middle1, n21, att1, wo1, ffn1)
+    g_ffn1 = share(half, owners_x)
+    dkv_own, dkv_oth, dq_pre = attend_back(q1, d_out, kp1, vp1, ot1, lse1)
+    terms = scatter_plane(dkv_own, after(dkv_oth, *g_ffn1[1:3]), g_ffn1[3:])
+    grad1, a_own, a_oth = project_back(
+        1, terms, dq_pre, normed1, stream1, wqkv1, mid_grad, *small
+    )
+
+    half_attn = add_cores(a_own, a_oth)
+    g_attn1 = share(half_attn, range(4))
+    d_out, half, mid_grad, small = ffn_back(
+        0, grad1, middle0, n20, att0, wo0, ffn0, [half_attn]
+    )
+    g_ffn0 = share(half, owners_x)
+    dkv_own, dkv_oth, dq_pre = attend_back(q0, after(d_out, *g_attn1), kp0, vp0, ot0, lse0)
+    terms = scatter_plane(dkv_own, after(dkv_oth, *g_ffn0[1:3]), g_ffn0[3:])
+    grad0, a_own, a_oth = project_back(
+        0, terms, dq_pre, normed0, stream0, wqkv0, mid_grad, *small
+    )
+    g_attn0 = share(add_cores(a_own, a_oth), range(4))
+
+    cut = call(
+        pack_kernel,
+        [((PACK // 4, D), BF)] * 4,
+        [place, *g_ffn0, *g_ffn1, *g_attn0, *g_attn1],
+        smem=1,
+        scratch=[pltpu.VMEM((PACK, D), BF)],
+        us=3.0,
+        name="pack",
+    )
+    piece = total(scatter_stage(cut, plane_one)).astype(BF)
+    piece = total(gather_stage(piece, plane_two)).astype(BF)
+    mine = gather_stage(piece, plane_one)
+    *grads, gain_sums = call(
+        unpack_kernel,
+        [
+            ((2, 144, D), F32),
+            ((2, 144, KW), F32),
+            ((2, 144, KW), F32),
+            ((2, 144, D), F32),
+            ((2, D, 384), F32),
+            ((2, D, 384), F32),
+            ((2, D, 384), F32),
+            ((16, D), F32),
+        ],
+        [place, *mine, *swap(mine)],
+        smem=1,
+        scratch=[pltpu.VMEM((PACK, D), BF), pltpu.VMEM((PACK, D), BF), pltpu.VMEM((384, D), F32)],
+        us=6.0,
+        name="unpack",
+    )
+    own_gains = lax.dynamic_slice_in_dim(gain_sums, 144 * x, 144, 1).reshape(2, 8, 144)
+    grads[6] = jnp.swapaxes(grads[6], 1, 2)
+    return (out.T[None], grad0.T[None], *grads, own_gains[:, 0], own_gains[:, 1])
 
 
 def solution(mesh):

time: 591 us -> 462 us (0.78)
  waiting for transfers between devices: 241 us -> 149 us
  other arithmetic: 42.6 us -> 17.1 us
  local copies, waits for them, and re-layouts: 54.4 us -> 29.2 us
  Pallas kernels: 129 us -> 149 us
    ppermute x89 -> x75, waiting for transfers between devices: 241 us -> 142 us  [send(): return lax.ppermute(value, AXES, pairs(move))]
    pallas_call x11 -> x15, Pallas kernels: 129 us -> 149 us  [call(): pl.pallas_call(body, out_shape=[jax.ShapeDtypeStruct(s, d) for s, d in ou...]
    another operation x12 -> x1, other arithmetic: 13.1 us -> 0.56 us  [local(): place = jnp.stack(spots).astype(jnp.int32)]
    convert_element_type x18 -> x8, other arithmetic: 18.1 us -> 8.92 us  [the longest x2 5.08 us: ffn_back(): half = total([g_own, g_oth]).astype(BF)]
    unnamed x104 -> x138, local copies, waits for them, and re-layouts: 19.3 us -> 11 us
    reshape x4 -> x1, local copies, waits for them, and re-layouts: 8.42 us -> 0.81 us  [local(): lax.dynamic_slice_in_dim(gain_sums, 144 * x, 144, 1).reshape(2, 8, 144)]
    all_gather x1 -> x2, waiting for transfers between devices: 0.01 us -> 6.34 us  [gather_ffn(): return lax.all_gather(mine, 'fsdp', axis=0)]
    ppermute x89 -> x75, starting transfers between devices: 100 us -> 94.2 us  [send(): return lax.ppermute(value, AXES, pairs(move))]
  transfers between devices with their start and end apart: 90 -> 77, of which waited for: 44 -> 47; matrix products, arithmetic and copies ran while one was open for 11% -> 4% of each run, Pallas kernels for 14% -> 23%
where the time goes in v2:
time: 462 us; the launch traced here: 453 us
  waiting for transfers between devices  149 us (32%)
  Pallas kernels  149 us (32%)
  starting transfers between devices  94.3 us (20%)
  local copies, waits for them, and re-layouts  29.2 us (6%)
  other arithmetic  17.1 us (4%)
  between operations  15 us (3%)
    pallas_call x15, Pallas kernels, call(): pl.pallas_call(body, out_shape=[jax.ShapeDtypeStruct(s, d) for s, d in ou...  149 us
    ppermute x75, waiting for transfers between devices, send(): return lax.ppermute(value, AXES, pairs(move))  142 us
    ppermute x75, starting transfers between devices, send(): return lax.ppermute(value, AXES, pairs(move))  94.2 us
    unnamed x138, local copies, waits for them, and re-layouts  11 us
  transfers between devices with their start and end apart: 77, of which 47 were waited for; matrix products, arithmetic and copies ran while one was open for 4% of the time, Pallas kernels for 23%

profile of v2, /device:TPU:1, one launch (start us, length us, event | category | flops | bytes accessed | tf_op | source)
XLA Modules:
  0.0 453.3 jit_solution(8932908422770252190)
XLA Ops:
  58.9 6.3 %all-gather.5.cloned.1.call-done = bf16[2304,576]{1,0:T(8,128)(2,1)} async-done(((bf16[576,576]{1,0:T(8,128)(2,1)}), bf16[2304,576]{1,0:T(8,128)(2,1)}) %all-gather.5.cloned.1.call-update) | async-done | bytes 2654224 | tf_op jit(solution)/shard_map/all_gather | solution.py:513
  75.4 18.1 %attend.2 = (bf16[4096,192]{1,0:T(8,128)(2,1)}, bf16[4096,192]{1,0:T(8,128)(2,1)}, f32[2,192,576]{2,1,0:T(8,128)}, f32[2,8,576]{2,1,0:T(8,128)}, bf16[128,576]{1,0:T(8,128)(2,1)}) custom-call(s32[64]{0:T(128)} %reshape.232.tab, s32[2]{0:T(128)} %get-tuple-element.174.own_pos, bf16[128,576]{1,0:T(8,128)(2,1)} %get-tuple-element.92.q, ...), custom_call_target="tpu_custom_call" | custom-call | flops 13200000000 | bytes 1000000 | tf_op jit(solution)/shard_map/attend/pallas_call | solution.py:133
  98.8 9.0 %middle_first.1 = (f32[128,576]{1,0:T(8,128)}, bf16[128,576]{1,0:T(8,128)(2,1)}, f32[128,576]{1,0:T(8,128)}, bf16[128,576]{1,0:T(8,128)(2,1)}, bf16[128,576]{1,0...) custom-call(s32[4]{0:T(128)} %pad_add_fusion.x_ref.place.place_ref, ...), custom_call_target="tpu_custom_call" | custom-call | flops 8800000000 | bytes 1000000 | tf_op jit(solution)/shard_map/middle_first/pallas_call | solution.py:133
  140.1 17.5 %attend.3 = (bf16[4096,192]{1,0:T(8,128)(2,1)}, bf16[4096,192]{1,0:T(8,128)(2,1)}, f32[2,192,576]{2,1,0:T(8,128)}, f32[2,8,576]{2,1,0:T(8,128)}, bf16[128,576]{1,0:T(8,128)(2,1)}) custom-call(s32[64]{0:T(128)} %reshape.232.tab, s32[2]{0:T(128)} %get-tuple-element.174.own_pos, bf16[128,576]{1,0:T(8,128)(2,1)} %get-tuple-element.103.q, ...), custom_call_target="tpu_custom_call" | custom-call | flops 13200000000 | bytes 1000000 | tf_op jit(solution)/shard_map/attend/pallas_call | solution.py:133
  157.6 7.1 %middle_last.1 = (f32[128,576]{1,0:T(8,128)}, bf16[128,576]{1,0:T(8,128)(2,1)}, f32[576,128]{1,0:T(8,128)}) custom-call(f32[128,576]{1,0:T(8,128)} %get-tuple-element.102.stream, bf16[128,576]{1,0:T(8,128)(2,1)} %get-tuple-element.105.att, bf16[576,576]{1,0:T(8,128)(2,1)} %get-tuple-element.106.wo, f32[8,576]{1,0:T(8,128)} %get-tuple-element.95.gains, ...), custom_call_target="tpu_custom_call" | custom-call | flops 6600000000 | bytes 1000000 | tf_op jit(solution)/shard_map/middle_last/pallas_call | solution.py:133
  164.7 6.8 %ffn_back_other.2 = (bf16[4,576,576]{2,1,0:T(8,128)(2,1)}, f32[128,576]{1,0:T(8,128)}) custom-call(f32[128,576]{1,0:T(8,128)} %bitcast.109, bf16[128,576]{1,0:T(8,128)(2,1)} %get-tuple-element.110.n2, bf16[4,576,576]{2,1,0:T(8,128)(2,1)} %collective-permute-done.31.v), custom_call_target="tpu_custom_call" | custom-call | flops 5500000256 | bytes 1000000 | tf_op jit(solution)/shard_map/ffn_back_other/pallas_call | solution.py:133
  171.6 8.1 %ffn_back_own.2 = (bf16[4,576,576]{2,1,0:T(8,128)(2,1)}, f32[128,576]{1,0:T(8,128)}, bf16[128,576]{1,0:T(8,128)(2,1)}, bf16[576,576]{1,0:T(8,128)(2,1)}, f32[8,576]{1,0:T(8,128)}) custom-call(f32[128,576]{1,0:T(8,128)} %bitcast.110, bf16[128,576]{1,0:T(8,128)(2,1)} %get-tuple-element.110.n2, bf16[4,576,576]{2,1,0:T(8,128)(2,1)} %bitcast.121, ...), custom_call_target="tpu_custom_call" | custom-call | flops 6600000000 | bytes 1000000 | tf_op jit(solution)/shard_map/ffn_back_own/pallas_call | solution.py:133
  187.4 20.7 %attend_back.2 = (bf16[2048,384]{1,0:T(8,128)(2,1)}, bf16[2048,384]{1,0:T(8,128)(2,1)}, bf16[128,576]{1,0:T(8,128)(2,1)}) custom-call(s32[64]{0:T(128)} %reshape.232.tab, s32[2]{0:T(128)} %get-tuple-element.174.own_pos, bf16[128,576]{1,0:T(8,128)(2,1)} %get-tuple-element.103.q, bf16[128,576]{1,0:T(8,128)(2,1)} %get-tuple-element.116.d_out, ...), custom_call_target="tpu_custom_call" | custom-call | flops 22000001024 | bytes 1000000 | tf_op jit(solution)/shard_map/attend_back/pallas_call | solution.py:133
  227.0 10.6 %collective-permute-done.39.refs_7_ = bf16[576,576]{1,0:T(8,128)(2,1)S(1)} collective-permute-done((bf16[576,576]{1,0:T(8,128)(2,1)S(1)}, bf16[576,576]{1,0:T(8,128)(2,1)S(1)}, u32[]{:S(2)}, u32[]{:S(2)}) %collective-permute-start.39) | collective-permute-done | bytes 663584 | tf_op jit(solution)/shard_map/ppermute | solution.py:59
  251.8 7.0 %ffn_back_other.3 = (bf16[4,576,576]{2,1,0:T(8,128)(2,1)}, f32[128,576]{1,0:T(8,128)}) custom-call(f32[128,576]{1,0:T(8,128)} %get-tuple-element.131.grad, bf16[128,576]{1,0:T(8,128)(2,1)} %get-tuple-element.132.n2, bf16[4,576,576]{2,1,0:T(8,128)(2,1)} %collective-permute-done.13.v), custom_call_target="tpu_custom_call" | custom-call | flops 5500000256 | bytes 1000000 | tf_op jit(solution)/shard_map/ffn_back_other/pallas_call | solution.py:133
  260.0 6.4 %collective-permute-done.43 = bf16[4,224,576]{2,1,0:T(8,128)(2,1)S(1)} collective-permute-done((bf16[4,224,576]{2,1,0:T(8,128)(2,1)S(1)}, bf16[4,224,576]{2,1,0:T(8,128)(2,1)S(1)}, u32[]{:S(2)}, u32[]{:S(2)}) %collective-permute-start.43) | collective-permute-done | bytes 1032224 | tf_op jit(solution)/shard_map/ppermute | solution.py:59
  272.1 8.0 %ffn_back_own.3 = (bf16[4,576,576]{2,1,0:T(8,128)(2,1)}, f32[128,576]{1,0:T(8,128)}, bf16[128,576]{1,0:T(8,128)(2,1)}, bf16[576,576]{1,0:T(8,128)(2,1)}, f32[8,576]{1,0:T(8,128)}) custom-call(f32[128,576]{1,0:T(8,128)} %get-tuple-element.131.grad, bf16[128,576]{1,0:T(8,128)(2,1)} %get-tuple-element.132.n2, bf16[4,576,576]{2,1,0:T(8,128)(2,1)} %bitcast.118, ...), custom_call_target="tpu_custom_call" | custom-call | flops 6600000000 | bytes 1000000 | tf_op jit(solution)/shard_map/ffn_back_own/pallas_call | solution.py:133
  287.4 20.5 %attend_back.3 = (bf16[2048,384]{1,0:T(8,128)(2,1)}, bf16[2048,384]{1,0:T(8,128)(2,1)}, bf16[128,576]{1,0:T(8,128)(2,1)}) custom-call(s32[64]{0:T(128)} %reshape.232.tab, s32[2]{0:T(128)} %get-tuple-element.174.own_pos, bf16[128,576]{1,0:T(8,128)(2,1)} %get-tuple-element.92.q, bf16[128,576]{1,0:T(8,128)(2,1)} %get-tuple-element.143.d_out, ...), custom_call_target="tpu_custom_call" | custom-call | flops 22000001024 | bytes 1000000 | tf_op jit(solution)/shard_map/attend_back/pallas_call | solution.py:133
  318.9 4.8 %collective-permute-done.53 = bf16[512,384]{1,0:T(8,128)(2,1)S(1)} collective-permute-done((bf16[512,384]{1,0:T(8,128)(2,1)S(1)}, bf16[512,384]{1,0:T(8,128)(2,1)S(1)}, u32[]{:S(2)}, u32[]{:S(2)}) %collective-permute-start.53) | collective-permute-done | bytes 393248 | tf_op jit(solution)/shard_map/ppermute | solution.py:59
  328.0 9.0 %collective-permute-done.54.refs_3_ = bf16[576,576]{1,0:T(8,128)(2,1)S(1)} collective-permute-done((bf16[576,576]{1,0:T(8,128)(2,1)S(1)}, bf16[576,576]{1,0:T(8,128)(2,1)S(1)}, u32[]{:S(2)}, u32[]{:S(2)}) %collective-permute-start.54) | collective-permute-done | bytes 663584 | tf_op jit(solution)/shard_map/ppermute | solution.py:59
  346.3 4.7 %project_back.3 = (f32[576,128]{1,0:T(8,128)}, bf16[4,224,576]{2,1,0:T(8,128)(2,1)}, bf16[4,224,576]{2,1,0:T(8,128)(2,1)}) custom-call(s32[4]{0:T(128)} %pad_add_fusion.x_ref.place.place_ref, bf16[128,384]{1,0:T(8,128)(2,1)} %get-tuple-element.206.t0, bf16[128,384]{1,0:T(8,128)(2,1)} %copy-done.55, bf16[128,384]{1,0:T(8,128)(2,1)} %copy-done.56, ...), custom_call_target="tpu_custom_call" | custom-call | flops 5500000256 | bytes 1000000 | tf_op jit(solution)/shard_map/project_back/pallas_call | solution.py:133
  360.9 5.6 %collective-permute-done.59.refs_9_ = bf16[224,576]{1,0:T(8,128)(2,1)S(1)} collective-permute-done((bf16[224,576]{1,0:T(8,128)(2,1)S(1)}, bf16[224,576]{1,0:T(8,128)(2,1)S(1)}, u32[]{:S(2)}, u32[]{:S(2)}) %collective-permute-start.59) | collective-permute-done | bytes 258080 | tf_op jit(solution)/shard_map/ppermute | solution.py:59
  366.6 8.3 %collective-permute-done.60.refs_10_ = bf16[224,576]{1,0:T(8,128)(2,1)S(1)} collective-permute-done((bf16[224,576]{1,0:T(8,128)(2,1)S(1)}, bf16[224,576]{1,0:T(8,128)(2,1)S(1)}, u32[]{:S(2)}, u32[]{:S(2)}) %collective-permute-start.60) | collective-permute-done | bytes 258080 | tf_op jit(solution)/shard_map/ppermute | solution.py:59
  375.6 6.6 %pack.1 = (bf16[400,576]{1,0:T(8,128)(2,1)}, bf16[400,576]{1,0:T(8,128)(2,1)}, bf16[400,576]{1,0:T(8,128)(2,1)}, bf16[400,576]{1,0:T(8,128)(2,1)}) custom-call(s32[4]{0:T(128)} %pad_add_fusion.x_ref.place.place_ref, bf16[576,576]{1,0:T(8,128)(2,1)} %get-tuple-element.179.refs_0_, bf16[576,576]{1,0:T(8,128)(2,1)} %copy-done.19, bf16[576,576]{1,0:T(8,128)(2,1)} %copy-done.20, ...), custom_call_target="tpu_custom_call" | custom-call | flops 3300000000 | bytes 1000000 | tf_op jit(solution)/shard_map/pack/pallas_call | solution.py:133
  385.8 6.4 %collective-permute-done.64 = bf16[400,576]{1,0:T(8,128)(2,1)S(1)} collective-permute-done((bf16[400,576]{1,0:T(8,128)(2,1)}, bf16[400,576]{1,0:T(8,128)(2,1)S(1)}, u32[]{:S(2)}, u32[]{:S(2)}) %collective-permute-start.64) | collective-permute-done | bytes 460832 | tf_op jit(solution)/shard_map/ppermute | solution.py:59
  392.2 5.4 %collective-permute-done.63 = bf16[400,576]{1,0:T(8,128)(2,1)S(1)} collective-permute-done((bf16[400,576]{1,0:T(8,128)(2,1)}, bf16[400,576]{1,0:T(8,128)(2,1)S(1)}, u32[]{:S(2)}, u32[]{:S(2)}) %collective-permute-start.63) | collective-permute-done | bytes 460832 | tf_op jit(solution)/shard_map/ppermute | solution.py:59
  401.2 7.6 %collective-permute-done.67 = bf16[400,576]{1,0:T(8,128)(2,1)S(1)} collective-permute-done((bf16[400,576]{1,0:T(8,128)(2,1)S(1)}, bf16[400,576]{1,0:T(8,128)(2,1)S(1)}, u32[]{:S(2)}, u32[]{:S(2)}) %collective-permute-start.67) | collective-permute-done | bytes 460832 | tf_op jit(solution)/shard_map/ppermute | solution.py:59
  424.0 9.6 %collective-permute-start.72 = (bf16[400,576]{1,0:T(8,128)(2,1)S(1)}, bf16[400,576]{1,0:T(8,128)(2,1)S(1)}, u32[]{:S(2)}, u32[]{:S(2)}) collective-permute-start(bf16[400,576]{1,0:T(8,128)(2,1)S(1)} %collective-permute-done.68.m1), channel_id=1, source_target_pairs={{0,4},{1,5},{2,6},{3,7},{4,0},{5,1},{6,2},{7,3},{8,12},{9,13},{10,... | collective-permute-start | bytes 1382408 | tf_op jit(solution)/shard_map/ppermute | solution.py:59
  436.7 7.6 %unpack.1 = (f32[2,144,576]{2,1,0:T(8,128)}, f32[2,144,192]{2,1,0:T(8,128)}, f32[2,144,192]{2,1,0:T(8,128)}, f32[2,144,576]{2,1,0:T(8,128)}, f32[2,576,384]{2,1,...) custom-call(s32[4]{0:T(128)} %pad_add_fusion.x_ref.place.place_ref, ...), custom_call_target="tpu_custom_call" | custom-call | flops 6600000000 | bytes 1000000 | tf_op jit(solution)/shard_map/unpack/pallas_call | solution.py:133
  (347 shorter events, 216.5 us)
Async XLA Ops:
  7.2 58.1 %all-gather.5.cloned.1.call-start = ((), (), s32[]{:S(2)}) async-start(), calls=%async_computation | async-start | bytes 3686400 | tf_op jit(solution)/shard_map/all_gather | solution.py:513
  23.7 96.3 %all-gather.7.cloned.1.call-start = ((), (), s32[]{:S(2)}) async-start(), calls=%async_computation.1 | async-start | bytes 3686400 | tf_op jit(solution)/shard_map/all_gather | solution.py:513
  65.3 32.8 %collective-permute-start.13 = (bf16[4,576,576]{2,1,0:T(8,128)(2,1)}, bf16[4,576,576]{2,1,0:T(8,128)(2,1)}, u32[]{:S(2)}, u32[]{:S(2)}) collective-permute-start(bf16[4,576,576]{2,1,0:T(8,128)(2,1)} %bitcast.116), channel_id=1, source_target_pairs={{0,4},{1,5},{2,6},{3,7},{4,0},{5,1},{6,2},{7,3},{8,12},{9,13},{10,... | collective-permute-start | bytes 7962632 | tf_op jit(solution)/shard_map/ppermute | solution.py:59
  71.5 23.3 %collective-permute-start.14 = (bf16[144,1152]{1,0:T(8,128)(2,1)S(1)}, bf16[144,1152]{1,0:T(8,128)(2,1)S(1)}, u32[]{:S(2)}, u32[]{:S(2)}) collective-permute-start(bf16[144,1152]{1,0:T(8,128)(2,1)S(1)} %maximum_select_fusion.r0), channel_id=1, source_target_pairs={{0,1},{1,2},{2,3},{3,0},{4,5},{5,6},{6,7},{7,4},{8,9},{9,10},{10,1... | collective-permute-start | bytes 995336 | tf_op jit(solution)/shard_map/ppermute | solution.py:59
  72.1 22.8 %collective-permute-start.15 = (bf16[144,1152]{1,0:T(8,128)(2,1)S(1)}, bf16[144,1152]{1,0:T(8,128)(2,1)S(1)}, u32[]{:S(2)}, u32[]{:S(2)}) collective-permute-start(bf16[144,1152]{1,0:T(8,128)(2,1)S(1)} %maximum_select_fusion.r0), channel_id=1, source_target_pairs={{0,3},{1,0},{2,1},{3,2},{4,7},{5,4},{6,5},{7,6},{8,11},{9,8},{10,9... | collective-permute-start | bytes 995336 | tf_op jit(solution)/shard_map/ppermute | solution.py:59
  74.2 21.1 %collective-permute-start.16 = (bf16[144,1152]{1,0:T(8,128)(2,1)S(1)}, bf16[144,1152]{1,0:T(8,128)(2,1)S(1)}, u32[]{:S(2)}, u32[]{:S(2)}) collective-permute-start(bf16[144,1152]{1,0:T(8,128)(2,1)S(1)} %maximum_select_fusion.r0), channel_id=1, source_target_pairs={{0,2},{1,3},{2,0},{3,1},{4,6},{5,7},{6,4},{7,5},{8,10},{9,11},{10,... | collective-permute-start | bytes 995336 | tf_op jit(solution)/shard_map/ppermute | solution.py:59
  129.4 28.2 %collective-permute-start.31 = (bf16[4,576,576]{2,1,0:T(8,128)(2,1)}, bf16[4,576,576]{2,1,0:T(8,128)(2,1)}, u32[]{:S(2)}, u32[]{:S(2)}) collective-permute-start(bf16[4,576,576]{2,1,0:T(8,128)(2,1)} %bitcast.119), channel_id=1, source_target_pairs={{0,4},{1,5},{2,6},{3,7},{4,0},{5,1},{6,2},{7,3},{8,12},{9,13},{10,... | collective-permute-start | bytes 7962632 | tf_op jit(solution)/shard_map/ppermute | solution.py:59
  183.4 24.7 %collective-permute-start.33 = (bf16[576,576]{1,0:T(8,128)(2,1)S(1)}, bf16[576,576]{1,0:T(8,128)(2,1)S(1)}, u32[]{:S(2)}, u32[]{:S(2)}) collective-permute-start(bf16[576,576]{1,0:T(8,128)(2,1)S(1)} %get-tuple-element.178), channel_id=1, source_target_pairs={{0,3},{1,0},{2,1},{3,2},{4,7},{5,4},{6,5},{7,6},{8,11},{9,8},{10,9... | collective-permute-start | bytes 1990664 | tf_op jit(solution)/shard_map/ppermute | solution.py:59
  187.4 20.7 %collective-permute-start.34 = (bf16[576,576]{1,0:T(8,128)(2,1)S(1)}, bf16[576,576]{1,0:T(8,128)(2,1)S(1)}, u32[]{:S(2)}, u32[]{:S(2)}) collective-permute-start(bf16[576,576]{1,0:T(8,128)(2,1)S(1)} %get-tuple-element.177), channel_id=1, source_target_pairs={{0,1},{1,2},{2,3},{3,0},{4,5},{5,6},{6,7},{7,4},{8,9},{9,10},{10,1... | collective-permute-start | bytes 1990664 | tf_op jit(solution)/shard_map/ppermute | solution.py:59
  218.3 19.3 %collective-permute-start.39 = (bf16[576,576]{1,0:T(8,128)(2,1)S(1)}, bf16[576,576]{1,0:T(8,128)(2,1)S(1)}, u32[]{:S(2)}, u32[]{:S(2)}) collective-permute-start(bf16[576,576]{1,0:T(8,128)(2,1)S(1)} %get-tuple-element.176), channel_id=1, source_target_pairs={{0,2},{1,3},{2,0},{3,1},{4,6},{5,7},{6,4},{7,5},{8,10},{9,11},{10,... | collective-permute-start | bytes 1990664 | tf_op jit(solution)/shard_map/ppermute | solution.py:59
  258.8 21.3 %collective-permute-start.44 = (bf16[4,576,576]{2,1,0:T(8,128)(2,1)}, bf16[4,576,576]{2,1,0:T(8,128)(2,1)S(1)}, u32[]{:S(2)}, u32[]{:S(2)}) collective-permute-start(bf16[4,576,576]{2,1,0:T(8,128)(2,1)} %get-tuple-element.141), channel_id=1, source_target_pairs={{0,4},{1,5},{2,6},{3,7},{4,0},{5,1},{6,2},{7,3},{8,12},{9,13},{10,... | collective-permute-start | bytes 7962632 | tf_op jit(solution)/shard_map/ppermute | solution.py:59
  267.6 16.2 %collective-permute-start.45 = (bf16[224,576]{1,0:T(8,128)(2,1)S(1)}, bf16[224,576]{1,0:T(8,128)(2,1)S(1)}, u32[]{:S(2)}, u32[]{:S(2)}) collective-permute-start(bf16[224,576]{1,0:T(8,128)(2,1)S(1)} %get-tuple-element.195), channel_id=1, source_target_pairs={{0,3},{1,0},{2,1},{3,2},{4,7},{5,4},{6,5},{7,6},{8,11},{9,8},{10,9... | collective-permute-start | bytes 774152 | tf_op jit(solution)/shard_map/ppermute | solution.py:59
  270.6 15.3 %collective-permute-start.46 = (bf16[224,576]{1,0:T(8,128)(2,1)S(1)}, bf16[224,576]{1,0:T(8,128)(2,1)S(1)}, u32[]{:S(2)}, u32[]{:S(2)}) collective-permute-start(bf16[224,576]{1,0:T(8,128)(2,1)S(1)} %get-tuple-element.194), channel_id=1, source_target_pairs={{0,1},{1,2},{2,3},{3,0},{4,5},{5,6},{6,7},{7,4},{8,9},{9,10},{10,1... | collective-permute-start | bytes 774152 | tf_op jit(solution)/shard_map/ppermute | solution.py:59
  270.6 15.3 %collective-permute-start.47 = (bf16[224,576]{1,0:T(8,128)(2,1)S(1)}, bf16[224,576]{1,0:T(8,128)(2,1)S(1)}, u32[]{:S(2)}, u32[]{:S(2)}) collective-permute-start(bf16[224,576]{1,0:T(8,128)(2,1)S(1)} %get-tuple-element.193), channel_id=1, source_target_pairs={{0,2},{1,3},{2,0},{3,1},{4,6},{5,7},{6,4},{7,5},{8,10},{9,11},{10,... | collective-permute-start | bytes 774152 | tf_op jit(solution)/shard_map/ppermute | solution.py:59
  285.9 22.1 %collective-permute-start.48 = (bf16[576,576]{1,0:T(8,128)(2,1)S(1)}, bf16[576,576]{1,0:T(8,128)(2,1)S(1)}, u32[]{:S(2)}, u32[]{:S(2)}) collective-permute-start(bf16[576,576]{1,0:T(8,128)(2,1)S(1)} %get-tuple-element.182), channel_id=1, source_target_pairs={{0,3},{1,0},{2,1},{3,2},{4,7},{5,4},{6,5},{7,6},{8,11},{9,8},{10,9... | collective-permute-start | bytes 1990664 | tf_op jit(solution)/shard_map/ppermute | solution.py:59
  286.3 21.7 %collective-permute-start.49 = (bf16[576,576]{1,0:T(8,128)(2,1)S(1)}, bf16[576,576]{1,0:T(8,128)(2,1)S(1)}, u32[]{:S(2)}, u32[]{:S(2)}) collective-permute-start(bf16[576,576]{1,0:T(8,128)(2,1)S(1)} %get-tuple-element.181), channel_id=1, source_target_pairs={{0,1},{1,2},{2,3},{3,0},{4,5},{5,6},{6,7},{7,4},{8,9},{9,10},{10,1... | collective-permute-start | bytes 1990664 | tf_op jit(solution)/shard_map/ppermute | solution.py:59
  318.6 18.4 %collective-permute-start.54 = (bf16[576,576]{1,0:T(8,128)(2,1)S(1)}, bf16[576,576]{1,0:T(8,128)(2,1)S(1)}, u32[]{:S(2)}, u32[]{:S(2)}) collective-permute-start(bf16[576,576]{1,0:T(8,128)(2,1)S(1)} %get-tuple-element.180), channel_id=1, source_target_pairs={{0,2},{1,3},{2,0},{3,1},{4,6},{5,7},{6,4},{7,5},{8,10},{9,11},{10,... | collective-permute-start | bytes 1990664 | tf_op jit(solution)/shard_map/ppermute | solution.py:59
  359.7 15.1 %collective-permute-start.60 = (bf16[224,576]{1,0:T(8,128)(2,1)S(1)}, bf16[224,576]{1,0:T(8,128)(2,1)S(1)}, u32[]{:S(2)}, u32[]{:S(2)}) collective-permute-start(bf16[224,576]{1,0:T(8,128)(2,1)S(1)} %get-tuple-element.190), channel_id=1, source_target_pairs={{0,1},{1,2},{2,3},{3,0},{4,5},{5,6},{6,7},{7,4},{8,9},{9,10},{10,1... | collective-permute-start | bytes 774152 | tf_op jit(solution)/shard_map/ppermute | solution.py:59
  360.0 14.8 %collective-permute-start.61 = (bf16[224,576]{1,0:T(8,128)(2,1)S(1)}, bf16[224,576]{1,0:T(8,128)(2,1)S(1)}, u32[]{:S(2)}, u32[]{:S(2)}) collective-permute-start(bf16[224,576]{1,0:T(8,128)(2,1)S(1)} %get-tuple-element.189), channel_id=1, source_target_pairs={{0,2},{1,3},{2,0},{3,1},{4,6},{5,7},{6,4},{7,5},{8,10},{9,11},{10,... | collective-permute-start | bytes 774152 | tf_op jit(solution)/shard_map/ppermute | solution.py:59
  382.7 14.9 %collective-permute-start.63 = (bf16[400,576]{1,0:T(8,128)(2,1)}, bf16[400,576]{1,0:T(8,128)(2,1)S(1)}, u32[]{:S(2)}, u32[]{:S(2)}) collective-permute-start(bf16[400,576]{1,0:T(8,128)(2,1)} %get-tuple-element.163), channel_id=1, source_target_pairs={{0,8},{1,9},{2,10},{3,11},{4,36},{5,37},{6,38},{7,39},{8,16},{9,17... | collective-permute-start | bytes 1382408 | tf_op jit(solution)/shard_map/ppermute | solution.py:59
  399.7 13.5 %collective-permute-start.66 = (bf16[400,576]{1,0:T(8,128)(2,1)S(1)}, bf16[400,576]{1,0:T(8,128)(2,1)S(1)}, u32[]{:S(2)}, u32[]{:S(2)}) collective-permute-start(bf16[400,576]{1,0:T(8,128)(2,1)S(1)} %add_convert_fusion.7), channel_id=1, source_target_pairs={{0,96},{1,97},{2,98},{3,99},{4,28},{5,29},{6,30},{7,31},{8,104},{9... | collective-permute-start | bytes 1382408 | tf_op jit(solution)/shard_map/ppermute | solution.py:59
  415.4 18.1 %collective-permute-start.69 = (bf16[400,576]{1,0:T(8,128)(2,1)S(1)}, bf16[400,576]{1,0:T(8,128)(2,1)S(1)}, u32[]{:S(2)}, u32[]{:S(2)}) collective-permute-start(bf16[400,576]{1,0:T(8,128)(2,1)S(1)} %add_convert_fusion.6.m0), channel_id=1, source_target_pairs={{0,24},{1,25},{2,26},{3,27},{4,100},{5,101},{6,102},{7,103},{8,0},... | collective-permute-start | bytes 1382408 | tf_op jit(solution)/shard_map/ppermute | solution.py:59
  417.2 16.4 %collective-permute-start.70 = (bf16[400,576]{1,0:T(8,128)(2,1)S(1)}, bf16[400,576]{1,0:T(8,128)(2,1)S(1)}, u32[]{:S(2)}, u32[]{:S(2)}) collective-permute-start(bf16[400,576]{1,0:T(8,128)(2,1)S(1)} %add_convert_fusion.6.m0), channel_id=1, source_target_pairs={{0,16},{1,17},{2,18},{3,19},{4,68},{5,69},{6,70},{7,71},{8,24},{9,... | collective-permute-start | bytes 1382408 | tf_op jit(solution)/shard_map/ppermute | solution.py:59
  417.6 16.6 %collective-permute-start.71 = (bf16[400,576]{1,0:T(8,128)(2,1)S(1)}, bf16[400,576]{1,0:T(8,128)(2,1)S(1)}, u32[]{:S(2)}, u32[]{:S(2)}) collective-permute-start(bf16[400,576]{1,0:T(8,128)(2,1)S(1)} %add_convert_fusion.6.m0), channel_id=1, source_target_pairs={{0,4},{1,5},{2,6},{3,7},{4,0},{5,1},{6,2},{7,3},{8,12},{9,13},{10,... | collective-permute-start | bytes 1382408 | tf_op jit(solution)/shard_map/ppermute | solution.py:59
  (114 other events, 842.1 us)
Sparse Core Ops, SparseCore 0:
  23.8 41.3 all-gather.4
  67.9 45.7 all-gather.6
